TPU v7x, 32 devices: a whole 2x2x4 slice. The times are simulated.
32 devices in a mesh: dp: 8 (over z, x), seq: 4 (over y, core).
Axes of the slice: x: 2, y: 2, z: 4, core: 2. Of those that a mesh axis runs over, the one named last changes fastest.
Arguments:
- tokens: bfloat16 [2, 8, 1536, 512], P(None, 'dp', 'seq'), may hold values from -6 to 6
- memory: bfloat16 [2, 8, 1024, 512], P(None, 'dp', 'seq'), may hold values from -6 to 6
- cotangent: bfloat16 [2, 8, 1536, 512], P(None, 'dp', 'seq'), may hold values from -6 to 6
- tgt_segments: int32 [2, 8, 1536], P(None, 'dp', 'seq'), may hold values from 0 to 7, never falling along the last dimension, each value on 1 to 768 neighbouring positions
- src_segments: int32 [2, 8, 1024], P(None, 'dp', 'seq'), may hold values from 0 to 7, never falling along the last dimension, each value on 1 to 512 neighbouring positions
- self_qkv: bfloat16 [512, 1536], P('dp'), may hold values from -0.375 to 0.375
- self_out: bfloat16 [512, 512], P('dp'), may hold values from -0.75 to 0.75
- cross_q: bfloat16 [512, 512], P('dp'), may hold values from -0.375 to 0.375
- cross_kv: bfloat16 [512, 1024], P('dp'), may hold values from -0.375 to 0.375
- cross_out: bfloat16 [512, 512], P('dp'), may hold values from -0.75 to 0.75
- ffn_up: bfloat16 [512, 2048], P('dp'), may hold values from -0.25 to 0.25
- ffn_down: bfloat16 [2048, 512], P('dp'), may hold values from -0.1875 to 0.1875
- proj_bias: bfloat16 [7, 512], P(None, 'dp'), may hold values from -1.796875 to 1.796875
- up_bias: bfloat16 [2048], P('dp'), may hold values from -1.796875 to 1.796875
- norm_gain: bfloat16 [3, 512], P(None, 'dp'), may hold values from 0.5 to 1.5
- norm_bias: bfloat16 [3, 512], P(None, 'dp'), may hold values from -1.796875 to 1.796875
Outputs:
- layer_out: bfloat16 [2, 8, 1536, 512], P(None, 'dp', 'seq')
- d_tokens: bfloat16 [2, 8, 1536, 512], P(None, 'dp', 'seq')
- d_memory: bfloat16 [2, 8, 1024, 512], P(None, 'dp', 'seq')
- grad_self_qkv: float32 [512, 1536], P('dp')
- grad_self_out: float32 [512, 512], P('dp')
- grad_cross_q: float32 [512, 512], P('dp')
- grad_cross_kv: float32 [512, 1024], P('dp')
- grad_cross_out: float32 [512, 512], P('dp')
- grad_ffn_up: float32 [512, 2048], P('dp')
- grad_ffn_down: float32 [2048, 512], P('dp')
- grad_proj_bias: float32 [7, 512], P(None, 'dp')
- grad_up_bias: float32 [2048], P('dp')
- grad_norm_gain: float32 [3, 512], P(None, 'dp')
- grad_norm_bias: float32 [3, 512], P(None, 'dp')
Inputs may be any that keep to these rules, and one draw needn't show every extreme that they name: `tgt_segments`: along a sequence the ids never fall; each of the 8 documents holds 1 to 768 target positions; target document k attends source document k. `src_segments`: along a sequence the ids never fall; each of the 8 documents holds 1 to 512 source positions.
All inputs are finite; a program needn't handle non-finite values.
Results may differ from a plain program's by a relative error of at most 0.024.
The roundings to bfloat16 on the way count: a program that leaves them out, or rounds other values in their place, can miss the bound.
Values may be sent and summed in bfloat16 or wider, within the bound.
A program may use at most 192 MiB of HBM per device.

v0:
```python
import math

import jax
import jax.numpy as jnp
from jax import lax
from jax.sharding import PartitionSpec as P

H = 8
MB = 2


def matmul(left, right):
    return jnp.dot(left, right, preferred_element_type=jnp.float32)


def outer_sum(left, right):
    return lax.dot_general(
        left, right, (((0,), (0,)), ((), ())), preferred_element_type=jnp.float32
    )


def times_transposed(grad_rows, weight):
    return lax.dot_general(
        grad_rows, weight, (((1,), (1,)), ((), ())), preferred_element_type=jnp.float32
    )


def gelu_parts(values):
    cumulative = 0.5 * (1.0 + lax.erf(values * 0.7071067811865476))
    density = jnp.exp(-0.5 * values * values) * 0.3989422804014327
    return (values * cumulative, cumulative + values * density)


def normalize(summed, gain, shift):
    center = summed - jnp.mean(summed, axis=-1, keepdims=True)
    scale_inv = lax.rsqrt(jnp.mean(center * center, axis=-1, keepdims=True) + 1e-05)
    unit_rows = center * scale_inv
    return (unit_rows * gain + shift, unit_rows, scale_inv)


def normalize_back(unit_rows, scale_inv, gain, grad_rows):
    scaled = grad_rows * gain
    back_rows = scale_inv * (
        scaled
        - jnp.mean(scaled, axis=-1, keepdims=True)
        - unit_rows * jnp.mean(scaled * unit_rows, axis=-1, keepdims=True)
    )
    return (back_rows, jnp.sum(grad_rows * unit_rows, axis=0), jnp.sum(grad_rows, axis=0))


def attend_forward(query_rows, key_rows, value_rows, query_ids, key_ids, local_heads):
    row_count = query_rows.shape[0]
    block_rows = min(512, row_count)
    block_count = row_count // block_rows
    head_size = query_rows.shape[1] // local_heads
    key_heads = key_rows.reshape(key_rows.shape[0], local_heads, head_size)
    value_heads = value_rows.reshape(value_rows.shape[0], local_heads, head_size)

    def one_block(pieces):
        query_block, block_ids = pieces
        scores = jnp.einsum(
            "qhd,khd->hqk",
            query_block.reshape(block_rows, local_heads, head_size),
            key_heads,
            preferred_element_type=jnp.float32,
        )
        scores = jnp.where((block_ids[:, None] == key_ids[None, :])[None], scores, -1e30)
        highest = jnp.max(scores, axis=-1, keepdims=True)
        weights = jnp.exp(scores - highest)
        row_total = jnp.sum(weights, axis=-1, keepdims=True)
        probs_low = (weights / row_total).astype(jnp.bfloat16)
        mixed_block = jnp.einsum(
            "hqk,khd->qhd", probs_low, value_heads, preferred_element_type=jnp.float32
        )
        return (
            mixed_block.reshape(block_rows, local_heads * head_size).astype(jnp.bfloat16),
            (highest + jnp.log(row_total))[:, :, 0],
        )

    mixed_blocks, spread = lax.map(
        one_block,
        (
            query_rows.reshape(block_count, block_rows, -1),
            query_ids.reshape(block_count, block_rows),
        ),
    )
    return (mixed_blocks.reshape(row_count, -1), spread)


def attend_backward(
    query_rows, key_rows, value_rows, grad_rows, spread, query_ids, key_ids, local_heads
):
    row_count = query_rows.shape[0]
    block_rows = min(512, row_count)
    block_count = row_count // block_rows
    head_size = query_rows.shape[1] // local_heads
    key_heads = key_rows.reshape(key_rows.shape[0], local_heads, head_size)
    value_heads = value_rows.reshape(value_rows.shape[0], local_heads, head_size)

    def one_block(carry, pieces):
        key_grad, value_grad = carry
        query_block, grad_block, spread_block, block_ids = pieces
        query_block = query_block.reshape(block_rows, local_heads, head_size)
        grad_block = grad_block.reshape(block_rows, local_heads, head_size)
        scores = jnp.einsum(
            "qhd,khd->hqk", query_block, key_heads, preferred_element_type=jnp.float32
        )
        scores = jnp.where((block_ids[:, None] == key_ids[None, :])[None], scores, -1e30)
        probs = jnp.exp(scores - spread_block[:, :, None])
        value_grad = value_grad + jnp.einsum(
            "hqk,qhd->khd",
            probs.astype(jnp.bfloat16),
            grad_block,
            preferred_element_type=jnp.float32,
        )
        prob_grad = jnp.einsum(
            "qhd,khd->hqk", grad_block, value_heads, preferred_element_type=jnp.float32
        )
        score_low = (
            probs * (prob_grad - jnp.sum(probs * prob_grad, axis=-1, keepdims=True))
        ).astype(jnp.bfloat16)
        query_grad = jnp.einsum(
            "hqk,khd->qhd", score_low, key_heads, preferred_element_type=jnp.float32
        )
        key_grad = key_grad + jnp.einsum(
            "hqk,qhd->khd", score_low, query_block, preferred_element_type=jnp.float32
        )
        return (
            (key_grad, value_grad),
            query_grad.reshape(block_rows, local_heads * head_size).astype(jnp.bfloat16),
        )

    empty_grad = jnp.zeros(key_heads.shape, jnp.float32)
    (key_grad, value_grad), query_grads = lax.scan(
        one_block,
        (empty_grad, empty_grad),
        (
            query_rows.reshape(block_count, block_rows, -1),
            grad_rows.reshape(block_count, block_rows, -1),
            spread,
            query_ids.reshape(block_count, block_rows),
        ),
    )
    key_rows_grad = key_grad.reshape(key_rows.shape[0], -1).astype(jnp.bfloat16)
    value_rows_grad = value_grad.reshape(value_rows.shape[0], -1).astype(jnp.bfloat16)
    return (query_grads.reshape(row_count, -1), key_rows_grad, value_rows_grad)


def fetch_each(shards):
    return (
        lax.all_gather(shards[0], "dp", axis=0, tiled=True),
        lax.all_gather(shards[1], "dp", axis=0, tiled=True),
        lax.all_gather(shards[2], "dp", axis=0, tiled=True),
        lax.all_gather(shards[3], "dp", axis=0, tiled=True),
        lax.all_gather(shards[4], "dp", axis=0, tiled=True),
        lax.all_gather(shards[5], "dp", axis=0, tiled=True),
        lax.all_gather(shards[6], "dp", axis=0, tiled=True),
        lax.all_gather(shards[7], "dp", axis=1, tiled=True),
        lax.all_gather(shards[8], "dp", axis=0, tiled=True),
        lax.all_gather(shards[9], "dp", axis=1, tiled=True),
        lax.all_gather(shards[10], "dp", axis=1, tiled=True),
    )


def settle(grads):
    shares = (
        lax.psum_scatter(grads[0], "dp", scatter_dimension=0, tiled=True),
        lax.psum_scatter(grads[1], "dp", scatter_dimension=0, tiled=True),
        lax.psum_scatter(grads[2], "dp", scatter_dimension=0, tiled=True),
        lax.psum_scatter(grads[3], "dp", scatter_dimension=0, tiled=True),
        lax.psum_scatter(grads[4], "dp", scatter_dimension=0, tiled=True),
        lax.psum_scatter(grads[5], "dp", scatter_dimension=0, tiled=True),
        lax.psum_scatter(grads[6], "dp", scatter_dimension=0, tiled=True),
        lax.psum_scatter(grads[7], "dp", scatter_dimension=1, tiled=True),
        lax.psum_scatter(grads[8], "dp", scatter_dimension=0, tiled=True),
        lax.psum_scatter(grads[9], "dp", scatter_dimension=1, tiled=True),
        lax.psum_scatter(grads[10], "dp", scatter_dimension=1, tiled=True),
    )
    return (
        lax.psum(shares[0].astype(jnp.bfloat16), "seq").astype(jnp.float32),
        lax.psum(shares[1].astype(jnp.bfloat16), "seq").astype(jnp.float32),
        lax.psum(shares[2].astype(jnp.bfloat16), "seq").astype(jnp.float32),
        lax.psum(shares[3].astype(jnp.bfloat16), "seq").astype(jnp.float32),
        lax.psum(shares[4].astype(jnp.bfloat16), "seq").astype(jnp.float32),
        lax.psum(shares[5].astype(jnp.bfloat16), "seq").astype(jnp.float32),
        lax.psum(shares[6].astype(jnp.bfloat16), "seq").astype(jnp.float32),
        lax.psum(shares[7].astype(jnp.bfloat16), "seq").astype(jnp.float32),
        lax.psum(shares[8].astype(jnp.bfloat16), "seq").astype(jnp.float32),
        lax.psum(shares[9].astype(jnp.bfloat16), "seq").astype(jnp.float32),
        lax.psum(shares[10].astype(jnp.bfloat16), "seq").astype(jnp.float32),
    )


def forward_pass(inputs, memory_rows, tgt_ids, src_ids, params, local_heads):
    w_qkv, w_out, w_query, w_pair, w_cross, w_up, w_down, biases, up_shift, gains, shifts = params
    model_width = inputs.shape[-1]
    bias_rows = biases.astype(jnp.float32)
    gain_rows = gains.astype(jnp.float32)
    shift_rows = shifts.astype(jnp.float32)
    packed = matmul(inputs, w_qkv)
    query_rows = ((packed[:, :model_width] + bias_rows[0]) * 0.125).astype(jnp.bfloat16)
    key_rows = packed[:, model_width : 2 * model_width].astype(jnp.bfloat16)
    value_rows = (packed[:, 2 * model_width :] + bias_rows[1]).astype(jnp.bfloat16)
    pair_rows = matmul(memory_rows, w_pair)
    cross_key = pair_rows[:, :model_width].astype(jnp.bfloat16)
    cross_value = (pair_rows[:, model_width:] + bias_rows[4]).astype(jnp.bfloat16)
    head_q, head_k, head_v, head_ck, head_cv = (
        lax.all_to_all(query_rows, "seq", split_axis=1, concat_axis=0, tiled=True),
        lax.all_to_all(key_rows, "seq", split_axis=1, concat_axis=0, tiled=True),
        lax.all_to_all(value_rows, "seq", split_axis=1, concat_axis=0, tiled=True),
        lax.all_to_all(cross_key, "seq", split_axis=1, concat_axis=0, tiled=True),
        lax.all_to_all(cross_value, "seq", split_axis=1, concat_axis=0, tiled=True),
    )
    self_heads, self_spread = attend_forward(head_q, head_k, head_v, tgt_ids, tgt_ids, local_heads)
    self_mixed = lax.all_to_all(self_heads, "seq", split_axis=0, concat_axis=1, tiled=True)
    first_norm, first_unit, first_scale = normalize(
        inputs.astype(jnp.float32) + (matmul(self_mixed, w_out) + bias_rows[2]),
        gain_rows[0],
        shift_rows[0],
    )
    first_low = first_norm.astype(jnp.bfloat16)
    cross_query = ((matmul(first_low, w_query) + bias_rows[3]) * 0.125).astype(jnp.bfloat16)
    head_cq = lax.all_to_all(cross_query, "seq", split_axis=1, concat_axis=0, tiled=True)
    cross_heads, cross_spread = attend_forward(
        head_cq, head_ck, head_cv, tgt_ids, src_ids, local_heads
    )
    cross_mixed = lax.all_to_all(cross_heads, "seq", split_axis=0, concat_axis=1, tiled=True)
    second, second_unit, second_scale = normalize(
        first_norm + (matmul(cross_mixed, w_cross) + bias_rows[5]), gain_rows[1], shift_rows[1]
    )
    second_low = second.astype(jnp.bfloat16)
    hidden = matmul(second_low, w_up) + up_shift.astype(jnp.float32)
    smooth, slope = gelu_parts(hidden)
    active = smooth.astype(jnp.bfloat16)
    third, third_unit, third_scale = normalize(
        second + (matmul(active, w_down) + bias_rows[6]), gain_rows[2], shift_rows[2]
    )
    saved = (
        inputs,
        memory_rows,
        tgt_ids,
        src_ids,
        head_q,
        head_k,
        head_v,
        head_ck,
        head_cv,
        head_cq,
        self_spread,
        cross_spread,
        self_mixed,
        cross_mixed,
        first_low,
        first_unit,
        first_scale,
        second_low,
        second_unit,
        second_scale,
        slope,
        active,
        third_unit,
        third_scale,
    )
    return (third.astype(jnp.bfloat16), saved)


def backward_pass(saved, grad_rows, params, local_heads):
    (
        inputs,
        memory_rows,
        tgt_ids,
        src_ids,
        head_q,
        head_k,
        head_v,
        head_ck,
        head_cv,
        head_cq,
        self_spread,
        cross_spread,
        self_mixed,
        cross_mixed,
        first_low,
        first_unit,
        first_scale,
        second_low,
        second_unit,
        second_scale,
        slope,
        active,
        third_unit,
        third_scale,
    ) = saved
    w_qkv, w_out, w_query, w_pair, w_cross, w_up, w_down, biases, up_shift, gains, shifts = params
    gain_rows = gains.astype(jnp.float32)
    grad_third, gain_grad2, shift_grad2 = normalize_back(
        third_unit, third_scale, gain_rows[2], grad_rows.astype(jnp.float32)
    )
    down_low = grad_third.astype(jnp.bfloat16)
    grad_down = outer_sum(active, down_low)
    up_low = (times_transposed(down_low, w_down) * slope).astype(jnp.bfloat16)
    grad_up = outer_sum(second_low, up_low)
    grad_second = grad_third + times_transposed(up_low, w_up)
    grad_mid, gain_grad1, shift_grad1 = normalize_back(
        second_unit, second_scale, gain_rows[1], grad_second
    )
    cross_low = grad_mid.astype(jnp.bfloat16)
    grad_cross = outer_sum(cross_mixed, cross_low)
    cross_grad = times_transposed(cross_low, w_cross).astype(jnp.bfloat16)
    head_cross_grad = lax.all_to_all(cross_grad, "seq", split_axis=1, concat_axis=0, tiled=True)
    cross_dq, cross_dk, cross_dv = attend_backward(
        head_cq, head_ck, head_cv, head_cross_grad, cross_spread, tgt_ids, src_ids, local_heads
    )
    token_dq, token_dk, token_dv = (
        lax.all_to_all(cross_dq, "seq", split_axis=0, concat_axis=1, tiled=True),
        lax.all_to_all(cross_dk, "seq", split_axis=0, concat_axis=1, tiled=True),
        lax.all_to_all(cross_dv, "seq", split_axis=0, concat_axis=1, tiled=True),
    )
    scaled_query = token_dq * 0.125
    grad_query = outer_sum(first_low, scaled_query)
    pair_grad = jnp.concatenate([token_dk, token_dv], axis=1)
    grad_pair = outer_sum(memory_rows, pair_grad)
    memory_grad = times_transposed(pair_grad, w_pair).astype(jnp.bfloat16)
    grad_first = grad_mid + times_transposed(scaled_query, w_query)
    grad_in, gain_grad0, shift_grad0 = normalize_back(
        first_unit, first_scale, gain_rows[0], grad_first
    )
    self_low = grad_in.astype(jnp.bfloat16)
    grad_out = outer_sum(self_mixed, self_low)
    self_grad = times_transposed(self_low, w_out).astype(jnp.bfloat16)
    head_self_grad = lax.all_to_all(self_grad, "seq", split_axis=1, concat_axis=0, tiled=True)
    self_dq, self_dk, self_dv = attend_backward(
        head_q, head_k, head_v, head_self_grad, self_spread, tgt_ids, tgt_ids, local_heads
    )
    own_dq, own_dk, own_dv = (
        lax.all_to_all(self_dq, "seq", split_axis=0, concat_axis=1, tiled=True),
        lax.all_to_all(self_dk, "seq", split_axis=0, concat_axis=1, tiled=True),
        lax.all_to_all(self_dv, "seq", split_axis=0, concat_axis=1, tiled=True),
    )
    scaled_self = own_dq * 0.125
    packed_grad = jnp.concatenate([scaled_self, own_dk, own_dv], axis=1)
    grad_qkv = outer_sum(inputs, packed_grad)
    input_grad = (grad_in + times_transposed(packed_grad, w_qkv)).astype(jnp.bfloat16)
    bias_grad = jnp.stack(
        [
            jnp.sum(scaled_self.astype(jnp.float32), axis=0),
            jnp.sum(own_dv.astype(jnp.float32), axis=0),
            jnp.sum(self_low.astype(jnp.float32), axis=0),
            jnp.sum(scaled_query.astype(jnp.float32), axis=0),
            jnp.sum(token_dv.astype(jnp.float32), axis=0),
            jnp.sum(cross_low.astype(jnp.float32), axis=0),
            jnp.sum(down_low.astype(jnp.float32), axis=0),
        ]
    )
    up_shift_grad = jnp.sum(up_low.astype(jnp.float32), axis=0)
    gain_grad = jnp.stack([gain_grad0, gain_grad1, gain_grad2])
    shift_grad = jnp.stack([shift_grad0, shift_grad1, shift_grad2])
    grads = (
        grad_qkv,
        grad_out,
        grad_query,
        grad_pair,
        grad_cross,
        grad_up,
        grad_down,
        bias_grad,
        up_shift_grad,
        gain_grad,
        shift_grad,
    )
    return (input_grad, memory_grad, grads)


def per_device(
    tokens,
    memory,
    cotangent,
    tgt_segments,
    src_segments,
    self_qkv,
    self_out,
    cross_q,
    cross_kv,
    cross_out,
    ffn_up,
    ffn_down,
    proj_bias,
    up_bias,
    norm_gain,
    norm_bias,
):
    shards = (
        self_qkv,
        self_out,
        cross_q,
        cross_kv,
        cross_out,
        ffn_up,
        ffn_down,
        proj_bias,
        up_bias,
        norm_gain,
        norm_bias,
    )
    local_heads = H // lax.axis_size("seq")
    tgt_full, src_full = (
        lax.all_gather(tgt_segments, "seq", axis=2, tiled=True),
        lax.all_gather(src_segments, "seq", axis=2, tiled=True),
    )
    grad_sums = None
    layer_rows = []
    input_grads = []
    memory_grads = []
    for micro_index in range(MB):
        forward_params = fetch_each(shards)
        output_rows, saved = forward_pass(
            tokens[micro_index, 0],
            memory[micro_index, 0],
            tgt_full[micro_index, 0],
            src_full[micro_index, 0],
            forward_params,
            local_heads,
        )
        backward_params = fetch_each(shards)
        input_grad, memory_grad, micro_grads = backward_pass(
            saved, cotangent[micro_index, 0], backward_params, local_heads
        )
        layer_rows.append(output_rows)
        input_grads.append(input_grad)
        memory_grads.append(memory_grad)
        grad_sums = (
            micro_grads if grad_sums is None else jax.tree.map(jnp.add, grad_sums, micro_grads)
        )
    grad_sums = settle(grad_sums)
    row_total = MB * lax.axis_size("dp") * tokens.shape[2] * lax.axis_size("seq")
    factor = 1.0 / math.sqrt(row_total)

    def rescale(grad_sum):
        return grad_sum * factor

    grad_sums = jax.tree.map(rescale, grad_sums)
    layer_out = jnp.stack(layer_rows)[:, None]
    d_tokens = jnp.stack(input_grads)[:, None]
    d_memory = jnp.stack(memory_grads)[:, None]
    return (
        layer_out,
        d_tokens,
        d_memory,
        grad_sums[0],
        grad_sums[1],
        grad_sums[2],
        grad_sums[3],
        grad_sums[4],
        grad_sums[5],
        grad_sums[6],
        grad_sums[7],
        grad_sums[8],
        grad_sums[9],
        grad_sums[10],
    )


def solution(mesh):
    placed = (
        P(None, "dp", "seq", None),
        P(None, "dp", "seq", None),
        P(None, "dp", "seq", None),
        P(None, "dp", "seq"),
        P(None, "dp", "seq"),
        P("dp", None),
        P("dp", None),
        P("dp", None),
        P("dp", None),
        P("dp", None),
        P("dp", None),
        P("dp", None),
        P(None, "dp"),
        P("dp"),
        P(None, "dp"),
        P(None, "dp"),
    )
    return jax.shard_map(
        per_device,
        mesh=mesh,
        in_specs=placed,
        out_specs=(
            P(None, "dp", "seq", None),
            P(None, "dp", "seq", None),
            P(None, "dp", "seq", None),
            P("dp", None),
            P("dp", None),
            P("dp", None),
            P("dp", None),
            P("dp", None),
            P("dp", None),
            P("dp", None),
            P(None, "dp"),
            P("dp"),
            P(None, "dp"),
            P(None, "dp"),
        ),
        check_vma=False,
    )
```

profile of v0, /device:TPU:0, one launch (start us, length us, event | category | flops | bytes accessed | tf_op | source)
XLA Modules:
  0.0 1514.3 jit_solution(18378178516953124394)
XLA Ops:
  9.4 28.1 %all-gather = bf16[8,64,7]{1,2,0:T(8,128)(2,1)S(1)} all-gather(bf16[1,64,7]{1,2,0:T(8,128)(2,1)} %bitcast.909), channel_id=1, replica_groups=mesh['dp'=8,'seq'=4] {'dp'}, dimensions={0}, use_global_device_ids=true | all-gather | bytes 8064 | tf_op jit(solution)/shard_map/all_gather | solution.py:158
  38.2 14.9 all-gather.11.cloned.1.call-done
  62.8 35.5 %all-gather.9.cloned.1.call-done = bf16[512,1536]{1,0:T(8,128)(2,1)} async-done(((bf16[64,1536]{1,0:T(8,128)(2,1)}), bf16[512,1536]{1,0:T(8,128)(2,1)}) %all-gather.9.cloned.1.call-update) | async-done | bytes 1572880 | tf_op jit(solution)/shard_map/all_gather | solution.py:151
  136.5 6.6 all-to-all-done.10
  147.2 18.4 %all-gather.1 = bf16[8,64,3]{1,2,0:T(4,128)(2,1)S(1)} all-gather(bf16[1,64,3]{1,2,0:T(4,128)(2,1)S(1)} %bitcast.912), channel_id=1, replica_groups=mesh['dp'=8,'seq'=4] {'dp'}, dimensions={0}, use_global_device_ids=true | all-gather | bytes 3456 | tf_op jit(solution)/shard_map/all_gather | solution.py:160
  171.0 16.4 %all-gather.2 = bf16[8,64,3]{1,2,0:T(4,128)(2,1)S(1)} all-gather(bf16[1,64,3]{1,2,0:T(4,128)(2,1)S(1)} %bitcast.913), channel_id=1, replica_groups=mesh['dp'=8,'seq'=4] {'dp'}, dimensions={0}, use_global_device_ids=true | all-gather | bytes 3456 | tf_op jit(solution)/shard_map/all_gather | solution.py:161
  193.4 7.7 all_gather.26
  207.0 7.6 all_gather.32
  214.6 31.2 %all_gather.29 = bf16[512,512]{1,0:T(8,128)(2,1)S(1)} all-gather(bf16[64,512]{1,0:T(8,128)(2,1)S(1)} %copy-done.108), channel_id=1, replica_groups=mesh['dp'=8,'seq'=4] {'dp'}, dimensions={0}, use_global_device_ids=true | all-gather | bytes 589824 | tf_op jit(solution)/shard_map/all_gather | solution.py:152
  255.4 24.8 %while.110 = (s32[]{:T(128)}, bf16[3,512,128]{2,1,0:T(8,128)(2,1)}, f32[3,2,512]{2,1,0:T(2,128)S(1)}, s32[3,512]{1,0:T(4,128)S(1)}, s32[1,1,1536]{2,1,0:T(1,128)...) while((s32[]{:T(128)}, bf16[3,512,128]{2,1,0:T(8,128)(2,1)}, ...), condition=%wide.region_17.18_spmd, body=%wide.region_14.17_spmd.sunk | while | flops 417659904 | bytes 23912576 | solution.py:80
  286.6 19.1 %while.108 = (s32[]{:T(128)}, bf16[3,512,128]{2,1,0:T(8,128)(2,1)}, f32[3,2,512]{2,1,0:T(2,128)S(1)}, s32[3,512]{1,0:T(4,128)S(1)}, s32[1,1,1536]{2,1,0:T(1,128)...) while((s32[]{:T(128)}, bf16[3,512,128]{2,1,0:T(8,128)(2,1)}, ...), condition=%wide.region_3.4_spmd, body=%wide.region_0.3_spmd.sunk | while | flops 417659904 | bytes 23912576 | solution.py:80
  309.3 33.4 %all_gather.33 = bf16[512,512]{1,0:T(8,128)(2,1)} all-gather(bf16[64,512]{1,0:T(8,128)(2,1)S(1)} %copy-done.109), channel_id=1, replica_groups=mesh['dp'=8,'seq'=4] {'dp'}, dimensions={0}, use_global_device_ids=true | all-gather | bytes 589824 | tf_op jit(solution)/shard_map/all_gather | solution.py:153
  370.1 14.1 while.109
  391.1 18.9 %while.111 = (s32[]{:T(128)}, bf16[3,512,128]{2,1,0:T(8,128)(2,1)}, f32[3,2,512]{2,1,0:T(2,128)S(1)}, s32[3,512]{1,0:T(4,128)}, s32[1,1,1024]{2,1,0:T(1,128)S(1)...) while((s32[]{:T(128)}, bf16[3,512,128]{2,1,0:T(8,128)(2,1)}, ...), condition=%wide.region_23.24_spmd, body=%wide.region_20.23_spmd.sunk | while | flops 278461440 | bytes 16296053 | solution.py:80
  413.5 18.3 %all-gather.3 = bf16[8,1,256]{2,1,0:T(2,128)(2,1)S(1)} all-gather(bf16[1,1,256]{2,1,0:T(2,128)(2,1)S(1)} %reshape.921), channel_id=1, replica_groups=mesh['dp'=8,'seq'=4] {'dp'}, dimensions={0}, use_global_device_ids=true | all-gather | bytes 4608 | tf_op jit(solution)/shard_map/all_gather | solution.py:159
  432.4 33.5 %all_gather.35 = bf16[512,512]{1,0:T(8,128)(2,1)} all-gather(bf16[64,512]{1,0:T(8,128)(2,1)S(1)} %copy-done.110), channel_id=1, replica_groups=mesh['dp'=8,'seq'=4] {'dp'}, dimensions={0}, use_global_device_ids=true | all-gather | bytes 589824 | tf_op jit(solution)/shard_map/all_gather | solution.py:155
  517.3 32.4 %while.114 = (s32[]{:T(128)}, f32[1024,2,64]{0,2,1:T(8,128)S(1)}, f32[1024,2,64]{0,2,1:T(8,128)S(1)}, bf16[3,512,128]{2,1,0:T(8,128)(2,1)}, bf16[3,512,128]{1,2,...) while((s32[]{:T(128)}, f32[1024,2,64]{0,2,1:T(8,128)S(1)}, ...), condition=%wide.region_46.47_spmd.clone, body=%wide.region_44.46_spmd.clone.sunk | while | flops 684784640 | bytes 38443168 | solution.py:134
  554.6 30.3 %while.112 = (s32[]{:T(128)}, f32[1024,2,64]{0,2,1:T(8,128)S(1)}, f32[1024,2,64]{0,2,1:T(8,128)S(1)}, bf16[3,512,128]{2,1,0:T(8,128)(2,1)}, bf16[3,512,128]{1,2,...) while((s32[]{:T(128)}, f32[1024,2,64]{0,2,1:T(8,128)S(1)}, ...), condition=%wide.region_34.35_spmd.clone, body=%wide.region_32.34_spmd.clone.sunk | while | flops 684784640 | bytes 38443168 | solution.py:134
  637.7 46.4 %while.115 = (s32[]{:T(128)}, f32[1536,2,64]{0,2,1:T(8,128)}, f32[1536,2,64]{0,2,1:T(8,128)}, bf16[3,512,128]{2,1,0:T(8,128)(2,1)}, bf16[3,512,128]{1,2,0:T(8,12...) while((s32[]{:T(128)}, f32[1536,2,64]{0,2,1:T(8,128)}, ...), condition=%wide.region_51.52_spmd.clone, body=%wide.region_49.51_spmd.clone.sunk | while | flops 1020853248 | bytes 55095460 | solution.py:134
  688.5 41.7 %while.113 = (s32[]{:T(128)}, f32[1536,2,64]{0,2,1:T(8,128)S(1)}, f32[1536,2,64]{0,2,1:T(8,128)}, bf16[3,512,128]{2,1,0:T(8,128)(2,1)}, bf16[3,512,128]{1,2,0:T(...) while((s32[]{:T(128)}, f32[1536,2,64]{0,2,1:T(8,128)S(1)}, ...), condition=%wide.region_39.40_spmd.clone, body=%wide.region_37.39_spmd.clone.sunk | while | flops 1020853248 | bytes 55095460 | solution.py:134
  758.4 6.0 all-to-all-done.27
  850.0 17.5 %all-reduce = bf16[2048]{0:T(1024)(128)(2,1)S(1)} all-reduce(f32[2048]{0:T(1024)S(1)} %add.536), channel_id=10, replica_groups=mesh['dp'=8,'seq'=4] {'dp'}, use_global_device_ids=true, to_apply=%region_84.85.clone | all-reduce | flops 2048 | bytes 12288
  879.3 44.8 %reduce-scatter.35.cloned.1.call-done = f32[64,7]{1,0:T(8,128)} async-done(((f32[512,7]{1,0:T(8,128)}), f32[64,7]{1,0:T(8,128)}) %reduce-scatter.35.cloned.1.call-update) | async-done | bytes 1808
  924.9 5.7 all-reduce.1
  931.2 58.7 %reduce-scatter.25.cloned.1.call-done = f32[64,512]{1,0:T(8,128)} async-done(((f32[512,512]{1,0:T(8,128)}), f32[64,512]{1,0:T(8,128)}) %reduce-scatter.25.cloned.1.call-update) | async-done | bytes 131088 | tf_op jit(solution)/shard_map/reduce_scatter | solution.py:171
  991.5 64.6 %reduce-scatter.23.cloned.1.call-done = f32[64,512]{1,0:T(8,128)} async-done(((f32[512,512]{1,0:T(8,128)}), f32[64,512]{1,0:T(8,128)}) %reduce-scatter.23.cloned.1.call-update) | async-done | bytes 131088 | tf_op jit(solution)/shard_map/reduce_scatter | solution.py:169
  1057.7 64.1 %reduce-scatter.21.cloned.1.call-done = f32[64,512]{1,0:T(8,128)} async-done(((f32[512,512]{1,0:T(8,128)}), f32[64,512]{1,0:T(8,128)}) %reduce-scatter.21.cloned.1.call-update) | async-done | bytes 131088 | tf_op jit(solution)/shard_map/reduce_scatter | solution.py:168
  1123.4 69.1 %reduce-scatter.33.cloned.1.call-done = f32[64,1024]{1,0:T(8,128)} async-done(((f32[512,1024]{1,0:T(8,128)}), f32[64,1024]{1,0:T(8,128)}) %reduce-scatter.33.cloned.1.call-update) | async-done | bytes 262160
  1194.3 75.4 %reduce-scatter.31.cloned.1.call-done = f32[64,1536]{1,0:T(8,128)} async-done(((f32[512,1536]{1,0:T(8,128)}), f32[64,1536]{1,0:T(8,128)}) %reduce-scatter.31.cloned.1.call-update) | async-done | bytes 393232
  1271.6 89.3 %reduce-scatter.27.cloned.1.call-done = f32[64,2048]{1,0:T(8,128)} async-done(((f32[512,2048]{1,0:T(8,128)}), f32[64,2048]{1,0:T(8,128)}) %reduce-scatter.27.cloned.1.call-update) | async-done | bytes 524304 | tf_op jit(solution)/shard_map/reduce_scatter | solution.py:172
  1362.7 89.4 %reduce-scatter.29.cloned.1.call-done = f32[256,512]{1,0:T(8,128)} async-done(((f32[2048,512]{1,0:T(8,128)}), f32[256,512]{1,0:T(8,128)}) %reduce-scatter.29.cloned.1.call-update) | async-done | bytes 524304 | tf_op jit(solution)/shard_map/reduce_scatter | solution.py:173
  1455.7 41.4 %all-reduce.5.cloned.1.call-done = (bf16[64,1536]{0,1:T(8,128)(2,1)}, bf16[64,512]{1,0:T(8,128)(2,1)}, bf16[64,512]{1,0:T(8,128)(2,1)}, bf16[64,1024]{0,1:T(8,12...) async-done(((bf16[64,1536]{0,1:T(8,128)(2,1)}, bf16[64,512]{1,0:T(8,128)(2,1)}, bf16[64,512]{1,0:T(8,128)(2,1)}, ...) | async-done | bytes 1048592 | tf_op jit(solution)/shard_map/psum | solution.py:180
  (937 shorter events, 617.9 us)
Async XLA Ops:
  7.2 45.9 %all-gather.11.cloned.1.call-start = ((), (), s32[]{:S(2)}) async-start(), calls=%async_computation.43 | async-start | bytes 1179648 | tf_op jit(solution)/shard_map/all_gather | solution.py:154
  7.9 90.3 %all-gather.9.cloned.1.call-start = ((), (), s32[]{:S(2)}) async-start(), calls=%async_computation.42 | async-start | bytes 1769472 | tf_op jit(solution)/shard_map/all_gather | solution.py:151
  8.7 463.4 %all-gather.13.cloned.1.call-start = ((), (), s32[]{:S(2)}) async-start(), calls=%async_computation.44 | async-start | bytes 2359296 | tf_op jit(solution)/shard_map/all_gather | solution.py:156
  55.7 46.2 %all-to-all-start.13 = ((bf16[256,4,128]{2,0,1:T(8,128)(2,1)}), bf16[256,4,128]{2,0,1:T(8,128)(2,1)S(1)}, u32[]{:S(2)}, u32[]{:S(2)}) async-start(bf16[256,4,128]{2,0,1:T(8,128)(2,1)} %copy_bitcast_fusion.13), calls=%async_computation.13 | async-start | bytes 524288 | tf_op jit(solution)/shard_map/all_to_all | solution.py:211
  143.1 24.3 %all-to-all-start.1 = ((bf16[384,4,128]{2,0,1:T(8,128)(2,1)}), bf16[384,4,128]{2,0,1:T(8,128)(2,1)S(1)}, u32[]{:S(2)}, u32[]{:S(2)}) async-start(bf16[384,4,128]{2,0,1:T(8,128)(2,1)} %copy_bitcast_fusion.10), calls=%async_computation.1 | async-start | bytes 786432 | tf_op jit(solution)/shard_map/all_to_all | solution.py:209
  146.6 330.2 %all-gather.15.cloned.1.call-start = ((), (), s32[]{:S(2)}) async-start(), calls=%async_computation.45 | async-start | bytes 2359296 | tf_op jit(solution)/shard_map/all_gather | solution.py:157
  167.4 21.8 %all-to-all-start.8 = ((bf16[384,4,128]{2,0,1:T(8,128)(2,1)}), bf16[384,4,128]{2,0,1:T(8,128)(2,1)S(1)}, u32[]{:S(2)}, u32[]{:S(2)}) async-start(bf16[384,4,128]{2,0,1:T(8,128)(2,1)} %bitcast.545), calls=%async_computation.8 | async-start | bytes 786432 | tf_op jit(solution)/shard_map/all_to_all | solution.py:208
  189.2 13.7 all-to-all-start
  202.9 48.3 %all-to-all-start.2 = ((bf16[384,4,128]{2,0,1:T(8,128)(2,1)}), bf16[384,4,128]{2,0,1:T(8,128)(2,1)S(1)}, u32[]{:S(2)}, u32[]{:S(2)}) async-start(bf16[384,4,128]{2,0,1:T(8,128)(2,1)} %bitcast.790), calls=%async_computation.2 | async-start | bytes 786432 | tf_op jit(solution)/shard_map/all_to_all | solution.py:210
  251.1 30.8 %all-to-all-start.14 = ((bf16[256,4,128]{2,0,1:T(8,128)(2,1)}), bf16[256,4,128]{2,0,1:T(8,128)(2,1)S(1)}, u32[]{:S(2)}, u32[]{:S(2)}) async-start(bf16[256,4,128]{2,0,1:T(8,128)(2,1)} %bitcast.549), calls=%async_computation.14 | async-start | bytes 524288 | tf_op jit(solution)/shard_map/all_to_all | solution.py:212
  281.9 23.8 %all-to-all-start.11 = ((bf16[4,384,128]{2,1,0:T(8,128)(2,1)}), bf16[4,384,128]{2,1,0:T(8,128)(2,1)S(1)}, u32[]{:S(2)}, u32[]{:S(2)}) async-start(bf16[4,384,128]{2,1,0:T(8,128)(2,1)} %bitcast.67), calls=%async_computation.11 | async-start | bytes 786432 | tf_op jit(solution)/shard_map/all_to_all | solution.py:215
  305.8 41.4 %all-to-all-start.3 = ((bf16[4,384,128]{2,1,0:T(8,128)(2,1)}), bf16[4,384,128]{2,1,0:T(8,128)(2,1)S(1)}, u32[]{:S(2)}, u32[]{:S(2)}) async-start(bf16[4,384,128]{2,1,0:T(8,128)(2,1)} %bitcast.32), calls=%async_computation.3 | async-start | bytes 786432 | tf_op jit(solution)/shard_map/all_to_all | solution.py:215
  364.0 20.2 %all-to-all-start.12 = ((bf16[384,4,128]{2,0,1:T(8,128)(2,1)}), bf16[384,4,128]{2,0,1:T(8,128)(2,1)}, u32[]{:S(2)}, u32[]{:S(2)}) async-start(bf16[384,4,128]{2,0,1:T(8,128)(2,1)} %bitcast.543), calls=%async_computation.12 | async-start | bytes 786432 | tf_op jit(solution)/shard_map/all_to_all | solution.py:223
  384.2 25.8 %all-to-all-start.7 = ((bf16[4,384,128]{2,1,0:T(8,128)(2,1)}), bf16[4,384,128]{2,1,0:T(8,128)(2,1)}, u32[]{:S(2)}, u32[]{:S(2)}) async-start(bf16[4,384,128]{2,1,0:T(8,128)(2,1)} %bitcast.798), calls=%async_computation.7 | async-start | bytes 786432 | tf_op jit(solution)/shard_map/all_to_all | solution.py:227
  410.0 57.8 %all-to-all-start.15 = ((bf16[4,384,128]{2,1,0:T(8,128)(2,1)}), bf16[4,384,128]{2,1,0:T(8,128)(2,1)S(1)}, u32[]{:S(2)}, u32[]{:S(2)}) async-start(bf16[4,384,128]{2,1,0:T(8,128)(2,1)} %bitcast.799), calls=%async_computation.15 | async-start | bytes 786432 | tf_op jit(solution)/shard_map/all_to_all | solution.py:227
  512.4 37.3 %all-to-all-start.16 = ((bf16[384,4,128]{2,0,1:T(8,128)(2,1)}), bf16[384,4,128]{2,0,1:T(8,128)(2,1)}, u32[]{:S(2)}, u32[]{:S(2)}) async-start(bf16[384,4,128]{2,0,1:T(8,128)(2,1)} %bitcast.542), calls=%async_computation.16 | async-start | bytes 786432 | tf_op jit(solution)/shard_map/all_to_all | solution.py:310
  549.7 35.2 %all-to-all-start.23 = ((bf16[4,384,128]{2,1,0:T(8,128)(2,1)}), bf16[4,384,128]{2,1,0:T(8,128)(2,1)}, u32[]{:S(2)}, u32[]{:S(2)}) async-start(bf16[4,384,128]{2,1,0:T(8,128)(2,1)} %bitcast.795), calls=%async_computation.23 | async-start | bytes 786432 | tf_op jit(solution)/shard_map/all_to_all | solution.py:315
  584.9 12.3 all-to-all-start.17
  597.2 13.6 all-to-all-start.29
  632.7 51.3 %all-to-all-start.18 = ((bf16[384,4,128]{2,0,1:T(8,128)(2,1)}), bf16[384,4,128]{2,0,1:T(8,128)(2,1)}, u32[]{:S(2)}, u32[]{:S(2)}) async-start(bf16[384,4,128]{2,0,1:T(8,128)(2,1)} %bitcast.541), calls=%async_computation.18 | async-start | bytes 786432 | tf_op jit(solution)/shard_map/all_to_all | solution.py:331
  684.1 46.2 %all-to-all-start.25 = ((bf16[4,384,128]{2,1,0:T(8,128)(2,1)}), bf16[4,384,128]{2,1,0:T(8,128)(2,1)S(1)}, u32[]{:S(2)}, u32[]{:S(2)}) async-start(bf16[4,384,128]{2,1,0:T(8,128)(2,1)} %bitcast.797), calls=%async_computation.25 | async-start | bytes 786432 | tf_op jit(solution)/shard_map/all_to_all | solution.py:336
  733.8 138.8 %reduce-scatter.39.cloned.1.call-start = ((), (), s32[]{:S(2)}) async-start(), calls=%async_computation.55 | async-start | bytes 294912
  745.3 128.1 %reduce-scatter.37.cloned.1.call-start = ((), (), s32[]{:S(2)}) async-start(), calls=%async_computation.54 | async-start | bytes 294912
  756.9 167.2 %reduce-scatter.35.cloned.1.call-start = ((), (), s32[]{:S(2)}) async-start(), calls=%async_computation.53 | async-start | bytes 294912
  768.0 222.0 %reduce-scatter.25.cloned.1.call-start = ((), (), s32[]{:S(2)}) async-start(), calls=%async_computation.48 | async-start | bytes 1179648 | tf_op jit(solution)/shard_map/reduce_scatter | solution.py:171
  770.9 285.3 %reduce-scatter.23.cloned.1.call-start = ((), (), s32[]{:S(2)}) async-start(), calls=%async_computation.47 | async-start | bytes 1179648 | tf_op jit(solution)/shard_map/reduce_scatter | solution.py:169
  775.5 346.3 %reduce-scatter.21.cloned.1.call-start = ((), (), s32[]{:S(2)}) async-start(), calls=%async_computation.46 | async-start | bytes 1179648 | tf_op jit(solution)/shard_map/reduce_scatter | solution.py:168
  793.3 399.2 %reduce-scatter.33.cloned.1.call-start = ((), (), s32[]{:S(2)}) async-start(), calls=%async_computation.52 | async-start | bytes 2359296
  820.4 449.3 %reduce-scatter.31.cloned.1.call-start = ((), (), s32[]{:S(2)}) async-start(), calls=%async_computation.51 | async-start | bytes 3538944
  834.2 526.7 %reduce-scatter.27.cloned.1.call-start = ((), (), s32[]{:S(2)}) async-start(), calls=%async_computation.49 | async-start | bytes 4718592 | tf_op jit(solution)/shard_map/reduce_scatter | solution.py:172
  841.7 610.5 %reduce-scatter.29.cloned.1.call-start = ((), (), s32[]{:S(2)}) async-start(), calls=%async_computation.50 | async-start | bytes 4718592 | tf_op jit(solution)/shard_map/reduce_scatter | solution.py:173
  848.1 649.0 %all-reduce.5.cloned.1.call-start = ((), (), s32[]{:S(2)}) async-start(), calls=%async_computation.56 | async-start | bytes 2752512 | tf_op jit(solution)/shard_map/psum | solution.py:180
  (176 other events, 2750.2 us)
Sparse Core Ops, SparseCore 0:
  10.1 42.8 all-gather.10
  55.3 42.9 all-gather.8
  100.4 48.0 all-gather.12
  150.5 48.0 all-gather.14
  738.0 58.9 reduce-scatter.38
  800.2 60.2 reduce-scatter.36
  863.8 60.2 reduce-scatter.34
  927.5 62.4 reduce-scatter.24
  993.8 62.3 reduce-scatter.22
  1059.4 62.3 reduce-scatter.20
  1125.8 66.6 reduce-scatter.32
  1196.4 73.3 reduce-scatter.30
  1273.8 87.1 reduce-scatter.26
  1364.5 87.6 reduce-scatter.28
  1456.3 40.8 all-reduce.4
where the time goes:
time: 1530 us; the launch traced here: 1510 us
  waiting for transfers between devices  708 us (46%)
  blocking collectives  218 us (14%)
  matrix products  215 us (14%)
  local copies, waits for them, and re-layouts  145 us (9%)
  starting transfers between devices  121 us (8%)
  other arithmetic  89.9 us (6%)
  between operations  17.3 us (1%)
    unnamed x20, waiting for transfers between devices  192 us
    reduce_scatter x1, waiting for transfers between devices, settle(): lax.psum_scatter(grads[6], 'dp', scatter_dimension=0, tiled=True)  89.4 us
    reduce_scatter x1, waiting for transfers between devices, settle(): lax.psum_scatter(grads[5], 'dp', scatter_dimension=0, tiled=True)  89.3 us
    reduce_scatter x1, waiting for transfers between devices, settle(): lax.psum_scatter(grads[2], 'dp', scatter_dimension=0, tiled=True)  64.6 us
    reduce_scatter x1, waiting for transfers between devices, settle(): lax.psum_scatter(grads[1], 'dp', scatter_dimension=0, tiled=True)  64.1 us
    reduce_scatter x1, waiting for transfers between devices, settle(): lax.psum_scatter(grads[4], 'dp', scatter_dimension=0, tiled=True)  58.7 us
    psum x1, waiting for transfers between devices, settle(): lax.psum(shares[0].astype(jnp.bfloat16), 'seq').astype(jnp.float32)  41.4 us
    dynamic_slice x72, local copies, waits for them, and re-layouts, attend_forward(): lax.map(one_block, (query_rows.reshape(block_count, block_rows, -1), quer...  37.6 us
  transfers between devices with their start and end apart: 47, of which 26 were waited for; matrix products, arithmetic and copies ran while one was open for 27% of the time, Pallas kernels for 0%

commit v1 on v0

v1 whole, which is shorter than its diff:
```python
import functools
import math

import jax
import jax.numpy as jnp
from jax import lax
from jax.experimental import pallas as pl
from jax.experimental.pallas import tpu as pltpu
from jax.sharding import PartitionSpec as P

H = 8
MB = 2
RB = 256
KB = 256
F32 = jnp.float32
BF16 = jnp.bfloat16


def mm(left, right):
    return jnp.dot(left, right, preferred_element_type=F32)


def mm_nt(left, right):
    return lax.dot_general(left, right, (((1,), (1,)), ((), ())), preferred_element_type=F32)


def mm_tn(left, right):
    return lax.dot_general(left, right, (((0,), (0,)), ((), ())), preferred_element_type=F32)


def gelu_parts(values):
    cumulative = 0.5 * (1.0 + lax.erf(values * 0.7071067811865476))
    density = jnp.exp(-0.5 * values * values) * 0.3989422804014327
    return values * cumulative, cumulative + values * density


def normalize(summed, gain, shift):
    center = summed - jnp.mean(summed, axis=-1, keepdims=True)
    scale_inv = lax.rsqrt(jnp.mean(center * center, axis=-1, keepdims=True) + 1e-05)
    unit_rows = center * scale_inv
    return unit_rows * gain + shift, unit_rows, scale_inv


def normalize_back(unit_rows, scale_inv, gain, grad_rows):
    scaled = grad_rows * gain
    return scale_inv * (
        scaled
        - jnp.mean(scaled, axis=-1, keepdims=True)
        - unit_rows * jnp.mean(scaled * unit_rows, axis=-1, keepdims=True)
    )


def fold(values, op):
    rows, cols = values.shape
    return op(values.reshape(rows // 8, 8, cols), axis=0)


def layer_kernel(
    bounds,
    x_hbm, m_hbm, ct_ref, vec_ref,
    wqkv_hbm, wout_hbm, wcq_hbm, wckv_hbm, wcout_hbm, wup_hbm, wdown_hbm,
    layer_out, mixed_out, self_low_out, first_low_out, cdq_out, cmixed_out, cross_low_out,
    second_low_out, up_low_out, active_out, down_low_out, dq_out, part_out,
    dkv_hbm, dckv_hbm, vecg_out,
    wqkv, wout, wcq, wckv, wcout, wup, wdown,
    xs, ms, k_s, kt_s, v_s, vt_s, k_c, kt_c, v_c, vt_c,
    p_s, p_c, dk_s, dv_s, dk_c, dv_c,
    qm_s, qm_c, gtm, gm, ot_s, ot_c, dqt, slope_s, sems,
):
    step = pl.program_id(0)
    steps = pl.num_programs(0)
    d_model = xs.shape[1]
    t_len = xs.shape[0]
    s_len = ms.shape[0]
    ff = wup.shape[1]
    hd = d_model // H
    core = bounds[0]
    block = 2 * step + core

    loads = [
        pltpu.make_async_copy(src, dst, sems.at[n])
        for n, (src, dst) in enumerate((
            (x_hbm, xs), (wqkv_hbm, wqkv), (m_hbm, ms), (wckv_hbm, wckv), (wout_hbm, wout), (wcq_hbm, wcq),
            (wcout_hbm, wcout), (wup_hbm, wup), (wdown_hbm, wdown),
        ))
    ]
    vec = vec_ref[...]

    @pl.when(step == 0)
    def _():
        for load in loads:
            load.start()
        dk_s[...] = jnp.zeros_like(dk_s)
        dv_s[...] = jnp.zeros_like(dv_s)
        dk_c[...] = jnp.zeros_like(dk_c)
        dv_c[...] = jnp.zeros_like(dv_c)
        vecg_out[...] = jnp.zeros_like(vecg_out)
        vec_t = vec.T

        def project(rows_ref, w_ref, k_at, kt, k, vt, v, bias_row, bias_row_t, count):
            wk = w_ref[:, k_at:k_at + d_model]
            wv = w_ref[:, k_at + d_model:k_at + 2 * d_model]
            wk_t = wk.T
            wv_t = wv.T

            def one(r, carry):
                at = pl.ds(pl.multiple_of(r * RB, RB), RB)
                rows = rows_ref[at, :]
                k[at, :] = mm(rows, wk).astype(BF16)
                v[at, :] = (mm(rows, wv) + bias_row).astype(BF16)
                kt[:, at] = mm_nt(wk_t, rows).astype(BF16)
                vt[:, at] = (mm_nt(wv_t, rows) + bias_row_t).astype(BF16)
                return carry

            lax.fori_loop(0, count // RB, one, 0)

        loads[0].wait()
        loads[1].wait()
        project(xs, wqkv, d_model, kt_s, k_s, vt_s, v_s, vec[1:2], vec_t[:, 1:2], t_len)
        loads[2].wait()
        loads[3].wait()
        project(ms, wckv, 0, kt_c, k_c, vt_c, v_c, vec[4:5], vec_t[:, 4:5], s_len)
        for load in loads[4:]:
            load.wait()

    qpos = block * RB + lax.broadcasted_iota(jnp.int32, (1, RB), 1)
    lo_s = jnp.zeros((1, RB), jnp.int32)
    hi_s = jnp.full((1, RB), bounds[2], jnp.int32)
    lo_c = jnp.zeros((1, RB), jnp.int32)
    hi_c = jnp.full((1, RB), bounds[2 + 8], jnp.int32)
    for doc in range(1, 8):
        inside = qpos >= bounds[1 + doc]
        lo_s = jnp.where(inside, bounds[1 + doc], lo_s)
        hi_s = jnp.where(inside, bounds[2 + doc], hi_s)
        lo_c = jnp.where(inside, bounds[9 + doc], lo_c)
        hi_c = jnp.where(inside, bounds[10 + doc], hi_c)
    first = block * RB
    last = first + RB - 1
    s_from, s_to, c_from, c_to = 0, bounds[2], 0, bounds[10]
    for doc in range(1, 8):
        in_first = first >= bounds[1 + doc]
        in_last = last >= bounds[1 + doc]
        s_from = jnp.where(in_first, bounds[1 + doc], s_from)
        c_from = jnp.where(in_first, bounds[9 + doc], c_from)
        s_to = jnp.where(in_last, bounds[2 + doc], s_to)
        c_to = jnp.where(in_last, bounds[10 + doc], c_to)

    def block_range(start, stop):
        return lax.div(start, KB), lax.div(stop + (KB - 1), KB)

    def halves(values, axis, h):
        place = lax.broadcasted_iota(jnp.int32, values.shape, axis)
        return jnp.where(place >= hd if h % 2 else place < hd, values, jnp.zeros_like(values))

    def put_masked(rows, rows_t, natural, transposed):
        for h in range(H):
            pair = slice((h // 2) * 2 * hd, (h // 2) * 2 * hd + 2 * hd)
            natural[h] = halves(rows[:, pair], 1, h)
            transposed[h] = halves(rows_t[pair, :], 0, h)

    def attend(qtm, k, vt, p, ot, lo, hi, start, stop):
        j_from, j_to = block_range(start, stop)

        def bias_of(j):
            kpos = j * KB + lax.broadcasted_iota(jnp.int32, (KB, RB), 0)
            return jnp.where((kpos >= lo) & (kpos < hi), 0.0, -1e30).astype(F32)

        def scores(h, at, bias):
            pair = slice((h // 2) * 2 * hd, (h // 2) * 2 * hd + 2 * hd)
            return mm(k[at, pair], qtm[h]) + bias

        def top(j, highest):
            at = pl.ds(pl.multiple_of(j * KB, KB), KB)
            bias = bias_of(j)
            return tuple(jnp.maximum(highest[h], fold(scores(h, at, bias), jnp.max)) for h in range(H))

        highest = lax.fori_loop(j_from, j_to, top, tuple(jnp.full((8, RB), -1e30, F32) for _ in range(H)))
        highest = [jnp.max(part, axis=0, keepdims=True) for part in highest]
        ot[...] = jnp.zeros_like(ot)

        def gather(j, totals):
            at = pl.ds(pl.multiple_of(j * KB, KB), KB)
            bias = bias_of(j)
            out = []
            for h in range(H):
                weights = jnp.exp(scores(h, at, bias) - highest[h])
                low = weights.astype(BF16)
                p[h, at, :] = low
                out.append(totals[h] + fold(weights, jnp.sum))
                head = slice(h * hd, (h + 1) * hd)
                ot[head, :] += mm(vt[head, at], low)
            return tuple(out)

        totals = lax.fori_loop(j_from, j_to, gather, tuple(jnp.zeros((8, RB), F32) for _ in range(H)))
        inverse = []
        for h in range(H):
            inv = 1.0 / jnp.sum(totals[h], axis=0, keepdims=True)
            head = slice(h * hd, (h + 1) * hd)
            ot[head, :] = ot[head, :] * inv
            inverse.append(inv)
        return inverse

    def attend_back(grad_rows, inverse, qm, k, kt, v, p, ot, dk, dv, start, stop):
        j_from, j_to = block_range(start, stop)
        grad_t = grad_rows.T.astype(F32)
        scaled_t = []
        spread = []
        for h in range(H):
            head = slice(h * hd, (h + 1) * hd)
            low_t = (grad_t[head] * inverse[h]).astype(BF16)
            scaled_t.append(low_t)
            spread.append(jnp.sum(ot[head, :] * low_t.astype(F32), axis=0, keepdims=True))
        scaled_t = jnp.concatenate(scaled_t, axis=0)
        put_masked(scaled_t.T, scaled_t, gm, gtm)
        dqt[...] = jnp.zeros_like(dqt)

        def body(j, carry):
            at = pl.ds(pl.multiple_of(j * KB, KB), KB)
            for pair_index in range(H // 2):
                pair = slice(pair_index * 2 * hd, (pair_index + 1) * 2 * hd)
                dk_part = None
                dv_part = None
                for h in (2 * pair_index, 2 * pair_index + 1):
                    low = p[h, at, :]
                    prob_grad = mm(v[at, pair], gtm[h])
                    score_low = (low.astype(F32) * (prob_grad - spread[h])).astype(BF16)
                    dv_h = mm(low, gm[h])
                    dk_h = mm(score_low, qm[h])
                    dv_part = dv_h if dv_part is None else dv_part + dv_h
                    dk_part = dk_h if dk_part is None else dk_part + dk_h
                    head = slice(h * hd, (h + 1) * hd)
                    dqt[head, :] += mm(kt[head, at], score_low)
                dk[at, pair] += dk_part
                dv[at, pair] += dv_part
            return carry

        lax.fori_loop(j_from, j_to, body, 0)
        return dqt[...].astype(BF16).T

    def add_vec(row, values):
        vecg_out[row:row + 1, :] += jnp.sum(values, axis=0, keepdims=True)

    x_rows = xs[pl.ds(pl.multiple_of(first, RB), RB), :]
    q = ((mm(x_rows, wqkv[:, :d_model]) + vec[0:1]) * 0.125).astype(BF16)
    put_masked(q, q.T, qm_s, gtm)
    inv_s = attend(gtm, k_s, vt_s, p_s, ot_s, lo_s, hi_s, s_from, s_to)
    mixed = ot_s[...].astype(BF16).T
    mixed_out[...] = mixed
    first_norm, unit1, scale1 = normalize(
        x_rows.astype(F32) + (mm(mixed, wout[...]) + vec[2:3]), vec[11:12], vec[14:15])
    first_low = first_norm.astype(BF16)
    first_low_out[...] = first_low
    cq = ((mm(first_low, wcq[...]) + vec[3:4]) * 0.125).astype(BF16)
    put_masked(cq, cq.T, qm_c, gtm)
    inv_c = attend(gtm, k_c, vt_c, p_c, ot_c, lo_c, hi_c, c_from, c_to)
    cmixed = ot_c[...].astype(BF16).T
    cmixed_out[...] = cmixed
    second, unit2, scale2 = normalize(
        first_norm + (mm(cmixed, wcout[...]) + vec[5:6]), vec[12:13], vec[15:16])
    second_low = second.astype(BF16)
    second_low_out[...] = second_low
    tile = d_model
    ffn = None
    for t in range(ff // tile):
        cols = slice(t * tile, (t + 1) * tile)
        hidden = mm(second_low, wup[:, cols]) + vec[7 + t:8 + t]
        smooth, slope = gelu_parts(hidden)
        active = smooth.astype(BF16)
        active_out[:, cols] = active
        slope_s[:, cols] = slope
        part = mm(active, wdown[cols, :])
        ffn = part if ffn is None else ffn + part
    third, unit3, scale3 = normalize(second + (ffn + vec[6:7]), vec[13:14], vec[16:17])
    layer_out[...] = third.astype(BF16)

    grad = ct_ref[...].astype(F32)
    add_vec(13, grad * unit3)
    add_vec(16, grad)
    grad_third = normalize_back(unit3, scale3, vec[13:14], grad)
    down_low = grad_third.astype(BF16)
    down_low_out[...] = down_low
    add_vec(6, down_low.astype(F32))
    back = grad_third
    for t in range(ff // tile):
        cols = slice(t * tile, (t + 1) * tile)
        up_low = (mm_nt(down_low, wdown[cols, :]) * slope_s[:, cols]).astype(BF16)
        up_low_out[:, cols] = up_low
        add_vec(7 + t, up_low.astype(F32))
        back = back + mm_nt(up_low, wup[:, cols])
    add_vec(12, back * unit2)
    add_vec(15, back)
    grad_mid = normalize_back(unit2, scale2, vec[12:13], back)
    cross_low = grad_mid.astype(BF16)
    cross_low_out[...] = cross_low
    add_vec(5, cross_low.astype(F32))
    cross_grad = mm_nt(cross_low, wcout[...]).astype(BF16)
    cdq = attend_back(cross_grad, inv_c, qm_c, k_c, kt_c, v_c, p_c, ot_c, dk_c, dv_c, c_from, c_to) * 0.125
    cdq_out[...] = cdq
    add_vec(3, cdq.astype(F32))
    grad_first = grad_mid + mm_nt(cdq, wcq[...])
    add_vec(11, grad_first * unit1)
    add_vec(14, grad_first)
    grad_in = normalize_back(unit1, scale1, vec[11:12], grad_first)
    self_low = grad_in.astype(BF16)
    self_low_out[...] = self_low
    add_vec(2, self_low.astype(F32))
    self_grad = mm_nt(self_low, wout[...]).astype(BF16)
    dq = attend_back(self_grad, inv_s, qm_s, k_s, kt_s, v_s, p_s, ot_s, dk_s, dv_s, s_from, s_to) * 0.125
    dq_out[...] = dq
    add_vec(0, dq.astype(F32))
    part_out[...] = grad_in + mm_nt(dq, wqkv[:, :d_model])

    @pl.when(step == steps - 1)
    def _():
        add_vec(1, dv_s[...])
        add_vec(4, dv_c[...])
        for n in range(2):
            cols = slice(n * 256, (n + 1) * 256)
            p_s[n] = dk_s[:, cols].astype(BF16)
            p_s[2 + n] = dv_s[:, cols].astype(BF16)
            p_c[n] = dk_c[:, cols].astype(BF16)
            p_c[2 + n] = dv_c[:, cols].astype(BF16)
        stores = [
            pltpu.make_async_copy(p_s.at[0:4], dkv_hbm, sems.at[0]),
            pltpu.make_async_copy(p_c.at[0:4], dckv_hbm, sems.at[1]),
        ]
        for store in stores:
            store.start()
        for store in stores:
            store.wait()


def run_layer(bounds, x_full, m_full, ct_full, vec, weights):
    t_len, d_model = x_full.shape
    s_len = m_full.shape[0]
    ff = weights[5].shape[1]
    steps = t_len // (2 * RB)
    own = t_len // 2
    any_spec = pl.BlockSpec(memory_space=pl.ANY)

    def rows(cols):
        return pl.BlockSpec((RB, cols), lambda i, b: (i, 0))

    def arr(cols, dtype=BF16):
        return jax.ShapeDtypeStruct((own, cols), dtype)

    out_shape = [arr(d_model) for _ in range(8)] + [arr(ff), arr(ff), arr(d_model), arr(d_model), arr(d_model, F32)]
    out_specs = [rows(s.shape[1]) for s in out_shape]
    out_shape += [
        jax.ShapeDtypeStruct((4, t_len, 256), BF16),
        jax.ShapeDtypeStruct((4, s_len, 256), BF16),
        jax.ShapeDtypeStruct((32, d_model), F32),
    ]
    out_specs += [any_spec, any_spec, pl.BlockSpec((32, d_model), lambda i, b: (0, 0))]
    bf = lambda *shape: pltpu.VMEM(shape, BF16)
    fl = lambda *shape: pltpu.VMEM(shape, F32)
    scratch = [bf(*w.shape) for w in weights] + [
        bf(t_len, d_model), bf(s_len, d_model),
        bf(t_len, d_model), bf(d_model, t_len), bf(t_len, d_model), bf(d_model, t_len),
        bf(s_len, d_model), bf(d_model, s_len), bf(s_len, d_model), bf(d_model, s_len),
        bf(H, t_len, RB), bf(H, s_len, RB),
        fl(t_len, d_model), fl(t_len, d_model), fl(s_len, d_model), fl(s_len, d_model),
        bf(H, RB, 128), bf(H, RB, 128), bf(H, 128, RB), bf(H, RB, 128),
        fl(d_model, RB), fl(d_model, RB), fl(d_model, RB), fl(RB, ff),
        pltpu.SemaphoreType.DMA((9,)),
    ]
    return pl.pallas_call(
        layer_kernel,
        out_shape=out_shape,
        grid_spec=pltpu.PrefetchScalarGridSpec(
            num_scalar_prefetch=1,
            grid=(steps,),
            in_specs=[any_spec, any_spec, pl.BlockSpec((RB, d_model), lambda i, b: (2 * i + b[0], 0)),
                      pl.BlockSpec((32, d_model), lambda i, b: (0, 0))] + [any_spec] * 7,
            out_specs=out_specs,
            scratch_shapes=scratch,
        ),
        compiler_params=pltpu.CompilerParams(vmem_limit_bytes=64 * 1024 * 1024 - 512 * 1024),
        name="layer",
    )(bounds, x_full, m_full, ct_full, vec, *weights)


def pack_vectors(proj_bias, up_bias, norm_gain, norm_bias, d_model):
    size, at = lax.axis_size("dp"), lax.axis_index("dp")
    width = d_model // size
    rows = jnp.concatenate([proj_bias, jnp.zeros((4, width), BF16), norm_gain, norm_bias], axis=0)
    packed = lax.dynamic_update_slice(jnp.zeros((32, d_model), BF16), rows, (0, at * width))
    flat = lax.dynamic_update_slice(jnp.zeros((4 * d_model,), BF16), up_bias, (at * up_bias.shape[0],))
    return lax.dynamic_update_slice(packed, flat.reshape(4, d_model), (7, 0))


def unpack_vectors(sums, d_model):
    size, at = lax.axis_size("dp"), lax.axis_index("dp")
    width = d_model // size
    own = lax.dynamic_slice(sums, (0, at * width), (32, width))
    up = lax.dynamic_slice(sums[7:11].reshape(-1), (at * 4 * width,), (4 * width,))
    return own[:7], up, own[11:14], own[14:17]


def gather_plain(tokens, memory, cotangent, counts, packed, shards):
    micro = lax.axis_index("seq") // MB

    def whole(rows):
        return lax.all_gather(lax.squeeze(rows, (1,)), "seq", axis=1, tiled=True)[micro]

    weights = [lax.all_gather(shard, "dp", axis=0, tiled=True) for shard in shards]
    vec = lax.psum(packed, "dp").astype(F32)
    bounds = lax.psum(counts, "seq")[micro]
    return whole(tokens), whole(memory), whole(cotangent), bounds, vec, weights


def own_rows(rows, core):
    blocks = rows.reshape(rows.shape[0] // (2 * RB), 2, RB, rows.shape[1])
    return blocks[:, core].reshape(rows.shape[0] // 2, rows.shape[1])


def spread_rows(rows, core):
    blocks = rows.reshape(rows.shape[0] // RB, 1, RB, rows.shape[1])
    blocks = jnp.concatenate([blocks, jnp.zeros_like(blocks)], axis=1)
    blocks = jnp.where(core == 0, blocks, blocks[:, ::-1])
    return blocks.reshape(rows.shape[0] * 2, rows.shape[1])


def settle_plain(x_full, m_full, weights, results, factor):
    (layer_rows, mixed, self_low, first_low, cdq, cmixed, cross_low, second_low, up_low, active, down_low, dq,
     part, dkv, dckv, vec_sums) = results
    place = lax.axis_index("seq")
    micro, core = place // MB, place % MB
    d_model = x_full.shape[1]
    dkv = jnp.moveaxis(dkv, 0, 1).reshape(x_full.shape[0], 2 * d_model)
    dckv = jnp.moveaxis(dckv, 0, 1).reshape(m_full.shape[0], 2 * d_model)
    input_rows = spread_rows(part, core) + mm_nt(dkv, weights[0][:, d_model:])
    memory_rows = mm_nt(dckv, weights[3])

    def home(rows):
        both = jnp.stack([rows, jnp.zeros_like(rows)])
        both = jnp.where(micro == 0, both, both[::-1])
        return lax.psum_scatter(both, "seq", scatter_dimension=1, tiled=True).astype(BF16)[:, None]

    grads = [
        jnp.concatenate([mm_tn(own_rows(x_full, core), dq), mm_tn(x_full, dkv)], axis=1),
        mm_tn(mixed, self_low), mm_tn(first_low, cdq), mm_tn(m_full, dckv), mm_tn(cmixed, cross_low),
        mm_tn(second_low, up_low), mm_tn(active, down_low),
    ]
    grads = [
        lax.psum(lax.psum_scatter(grad, "dp", scatter_dimension=0, tiled=True), "seq") * factor for grad in grads
    ]
    vec_sums = lax.psum(vec_sums, ("dp", "seq")) * factor
    return (home(spread_rows(layer_rows.astype(F32), core)), home(input_rows), home(memory_rows), *grads,
            *unpack_vectors(vec_sums, d_model))


def per_device(
    tokens, memory, cotangent, tgt_segments, src_segments,
    self_qkv, self_out, cross_q, cross_kv, cross_out, ffn_up, ffn_down, proj_bias, up_bias, norm_gain, norm_bias,
):
    d_model = tokens.shape[3]
    place = lax.axis_index("seq")
    core = place % MB
    shards = (self_qkv, self_out, cross_q, cross_kv, cross_out, ffn_up, ffn_down)
    docs = jnp.arange(9)
    tgt_counts = jnp.sum(tgt_segments[:, 0, :, None] < docs, axis=1, dtype=jnp.int32)
    src_counts = jnp.sum(src_segments[:, 0, :, None] < docs[1:], axis=1, dtype=jnp.int32)
    counts = jnp.concatenate([tgt_counts, src_counts], axis=1)
    packed = pack_vectors(proj_bias, up_bias, norm_gain, norm_bias, d_model)
    x_full, m_full, ct_full, bounds, vec, weights = gather_plain(
        tokens, memory, cotangent, counts, packed, shards)
    bounds = jnp.concatenate([core.astype(jnp.int32)[None], bounds, jnp.zeros((2,), jnp.int32)])
    results = run_layer(bounds, x_full, m_full, ct_full, vec, weights)
    row_total = MB * lax.axis_size("dp") * tokens.shape[2] * lax.axis_size("seq")
    return settle_plain(x_full, m_full, weights, results, 1.0 / math.sqrt(row_total))


def solution(mesh):
    rows = P(None, "dp", "seq", None)
    ids = P(None, "dp", "seq")
    sharded = P("dp", None)
    columns = P(None, "dp")
    return jax.shard_map(
        per_device,
        mesh=mesh,
        in_specs=(rows, rows, rows, ids, ids) + (sharded,) * 7 + (columns, P("dp"), columns, columns),
        out_specs=(rows, rows, rows) + (sharded,) * 7 + (columns, P("dp"), columns, columns),
        check_vma=False,
    )
```

time: 1530 us -> 1290 us (0.84)
  waiting for transfers between devices: 708 us -> 944 us
  matrix products: 215 us -> 24.6 us
  starting transfers between devices: 121 us -> 1.01 us
  local copies, waits for them, and re-layouts: 145 us -> 32.8 us
  Pallas kernels: 0 us -> 88.2 us
  blocking collectives: 218 us -> 145 us
  other arithmetic: 89.9 us -> 33.2 us
    reduce_scatter x5 -> x10, waiting for transfers between devices: 366 us -> 662 us  [the longest x7 507 us: settle_plain(): lax.psum_scatter(grad, 'dp', scatter_dimension=0, tiled=True)]
    dot_general x126 -> x10, matrix products: 215 us -> 24.6 us  [the longest x8 21.4 us: mm_tn(): lax.dot_general(left, right, (((0,), (0,)), ((), ())), preferred_element_...]
    unnamed x20 -> x19, waiting for transfers between devices: 192 us -> 5.04 us
    psum x1 -> x2, waiting for transfers between devices: 41.4 us -> 162 us  [the longest x1 109 us: settle_plain(): vec_sums = lax.psum(vec_sums, ('dp', 'seq')) * factor]
    all_to_all x32 -> x0, starting transfers between devices: 120 us -> none  [the longest x2 8.77 us: backward_pass(): lax.all_to_all(cross_dq, 'seq', split_axis=0, concat_axis=1, tiled=True)]
    all_gather x9 -> x3, blocking collectives: 195 us -> 101 us  [gather_plain(): lax.all_gather(shard, 'dp', axis=0, tiled=True)]
    pallas_call x0 -> x1, Pallas kernels: none -> 88.2 us  [run_layer(): pl.pallas_call(layer_kernel, out_shape=out_shape, grid_spec=pltpu.Prefetc...]
    all_gather x4 -> x7, waiting for transfers between devices: 50.4 us -> 114 us  [the longest x4 114 us: gather_plain(): lax.all_gather(shard, 'dp', axis=0, tiled=True)]
  transfers between devices with their start and end apart: 47 -> 19, of which waited for: 26 -> 15; matrix products, arithmetic and copies ran while one was open for 27% -> 6% of each run, Pallas kernels for 0% -> 0%
where the time goes in v1:
time: 1290 us; the launch traced here: 1280 us
  waiting for transfers between devices  944 us (73%)
  blocking collectives  145 us (11%)
  Pallas kernels  88.2 us (7%)
  other arithmetic  33.2 us (3%)
  local copies, waits for them, and re-layouts  32.8 us (3%)
  matrix products  24.6 us (2%)
  between operations  14.9 us (1%)
    reduce_scatter x7, waiting for transfers between devices, settle_plain(): lax.psum_scatter(grad, 'dp', scatter_dimension=0, tiled=True)  507 us
    reduce_scatter x3, waiting for transfers between devices, home(): lax.psum_scatter(both, 'seq', scatter_dimension=1, tiled=True).astype(BF16)  155 us
    all_gather x4, waiting for transfers between devices, gather_plain(): lax.all_gather(shard, 'dp', axis=0, tiled=True)  114 us
    psum x1, waiting for transfers between devices, settle_plain(): vec_sums = lax.psum(vec_sums, ('dp', 'seq')) * factor  109 us
    all_gather x3, blocking collectives, gather_plain(): lax.all_gather(shard, 'dp', axis=0, tiled=True)  101 us
    pallas_call x1, Pallas kernels, run_layer(): pl.pallas_call(layer_kernel, out_shape=out_shape, grid_spec=pltpu.Prefetc...  88.2 us
    psum x1, waiting for transfers between devices, settle_plain(): lax.psum(lax.psum_scatter(grad, 'dp', scatter_dimension=0, tiled=True), '...  53.2 us
    psum x1, blocking collectives, gather_plain(): vec = lax.psum(packed, 'dp').astype(F32)  39.1 us
  transfers between devices with their start and end apart: 19, of which 15 were waited for; matrix products, arithmetic and copies ran while one was open for 6% of the time, Pallas kernels for 0%

profile of v1, /device:TPU:0, one launch (start us, length us, event | category | flops | bytes accessed | tf_op | source)
XLA Modules:
  0.0 1283.6 jit_solution(14129447024858867900)
XLA Ops:
  16.2 39.1 %psum.71 = bf16[32,512]{1,0:T(8,128)(2,1)S(1)} all-reduce(bf16[32,512]{1,0:T(8,128)(2,1)S(1)} %dynamic_update_slice.11), channel_id=1, replica_groups=mesh['dp'=8,'seq'=4] {'dp'}, use_global_device_ids=true, to_apply=%region_3.4 | all-reduce | flops 16384 | bytes 65536 | tf_op jit(solution)/shard_map/psum | solution.py:407
  56.2 5.0 psum.70
  61.8 33.7 %all_gather.34.wout_hbm = bf16[512,512]{1,0:T(8,128)(2,1)} all-gather(bf16[64,512]{1,0:T(8,128)(2,1)S(1)} %copy-done.15), channel_id=1, replica_groups=mesh['dp'=8,'seq'=4] {'dp'}, dimensions={0}, use_global_device_ids=true | all-gather | bytes 589824 | tf_op jit(solution)/shard_map/all_gather | solution.py:406
  95.5 34.0 %all_gather.35.wcq_hbm = bf16[512,512]{1,0:T(8,128)(2,1)} all-gather(bf16[64,512]{1,0:T(8,128)(2,1)S(1)} %copy-done.16), channel_id=1, replica_groups=mesh['dp'=8,'seq'=4] {'dp'}, dimensions={0}, use_global_device_ids=true | all-gather | bytes 589824 | tf_op jit(solution)/shard_map/all_gather | solution.py:406
  129.5 33.6 %all_gather.37.wcout_hbm = bf16[512,512]{1,0:T(8,128)(2,1)} all-gather(bf16[64,512]{1,0:T(8,128)(2,1)S(1)} %copy-done.17), channel_id=1, replica_groups=mesh['dp'=8,'seq'=4] {'dp'}, dimensions={0}, use_global_device_ids=true | all-gather | bytes 589824 | tf_op jit(solution)/shard_map/all_gather | solution.py:406
  165.3 2.7 dynamic-slice_bitcast_fusion.ct_ref
  168.0 2.7 fusion.32.x_hbm
  170.7 14.4 %all-gather.11.cloned.1.call-done.wqkv_hbm = bf16[512,1536]{1,0:T(8,128)(2,1)} async-done(((bf16[64,1536]{1,0:T(8,128)(2,1)}), bf16[512,1536]{1,0:T(8,128)(2,1)}) %all-gather.11.cloned.1.call-update) | async-done | bytes 1572880 | tf_op jit(solution)/shard_map/all_gather | solution.py:406
  185.1 50.1 %all-gather.15.cloned.1.call-done.wup_hbm = bf16[512,2048]{1,0:T(8,128)(2,1)} async-done(((bf16[64,2048]{1,0:T(8,128)(2,1)}), bf16[512,2048]{1,0:T(8,128)(2,1)}) %all-gather.15.cloned.1.call-update) | async-done | bytes 2097168 | tf_op jit(solution)/shard_map/all_gather | solution.py:406
  235.2 49.9 %all-gather.17.cloned.1.call-done.wdown_hbm = bf16[2048,512]{1,0:T(8,128)(2,1)} async-done(((bf16[256,512]{1,0:T(8,128)(2,1)}), bf16[2048,512]{1,0:T(8,128)(2,1)}) %all-gather.17.cloned.1.call-update) | async-done | bytes 2097168 | tf_op jit(solution)/shard_map/all_gather | solution.py:406
  285.2 88.2 %layer.1 = (bf16[768,512]{1,0:T(8,128)(2,1)}, bf16[768,512]{1,0:T(8,128)(2,1)}, bf16[768,512]{1,0:T(8,128)(2,1)}, bf16[768,512]{1,0:T(8,128)(2,1)}, bf16[768,512...) custom-call(s32[20]{0:T(128)} %pad_add_fusion.1.bounds, ...), custom_call_target="tpu_custom_call" | custom-call | tf_op jit(solution)/shard_map/layer/pallas_call | solution.py:367
  373.4 3.2 fusion.8
  380.0 3.1 copy.66
  383.1 2.6 fusion.10
  385.9 3.2 copy.65
  389.1 2.7 constant_dynamic-slice_fusion.2
  398.1 4.9 fusion.12
  404.9 5.1 fusion.13
  417.7 44.5 %reduce-scatter.19.cloned.1.call-done = f32[64,512]{1,0:T(8,128)} async-done(((f32[512,512]{1,0:T(8,128)}), f32[64,512]{1,0:T(8,128)}) %reduce-scatter.19.cloned.1.call-update) | async-done | bytes 131088 | tf_op jit(solution)/shard_map/reduce_scatter | solution.py:446
  462.1 66.2 %reduce-scatter.21.cloned.1.call-done = f32[64,512]{1,0:T(8,128)} async-done(((f32[512,512]{1,0:T(8,128)}), f32[64,512]{1,0:T(8,128)}) %reduce-scatter.21.cloned.1.call-update) | async-done | bytes 131088 | tf_op jit(solution)/shard_map/reduce_scatter | solution.py:446
  528.3 65.8 %reduce-scatter.25.cloned.1.call-done = f32[64,512]{1,0:T(8,128)} async-done(((f32[512,512]{1,0:T(8,128)}), f32[64,512]{1,0:T(8,128)}) %reduce-scatter.25.cloned.1.call-update) | async-done | bytes 131088 | tf_op jit(solution)/shard_map/reduce_scatter | solution.py:446
  594.2 70.9 %reduce-scatter.23.cloned.1.call-done = f32[64,1024]{1,0:T(8,128)} async-done(((f32[512,1024]{1,0:T(8,128)}), f32[64,1024]{1,0:T(8,128)}) %reduce-scatter.23.cloned.1.call-update) | async-done | bytes 262160 | tf_op jit(solution)/shard_map/reduce_scatter | solution.py:446
  665.1 77.1 %reduce-scatter.17.cloned.1.call-done = f32[64,1536]{1,0:T(8,128)} async-done(((f32[512,1536]{1,0:T(8,128)}), f32[64,1536]{1,0:T(8,128)}) %reduce-scatter.17.cloned.1.call-update) | async-done | bytes 393232 | tf_op jit(solution)/shard_map/reduce_scatter | solution.py:446
  742.2 91.2 %reduce-scatter.27.cloned.1.call-done = f32[64,2048]{1,0:T(8,128)} async-done(((f32[512,2048]{1,0:T(8,128)}), f32[64,2048]{1,0:T(8,128)}) %reduce-scatter.27.cloned.1.call-update) | async-done | bytes 524304 | tf_op jit(solution)/shard_map/reduce_scatter | solution.py:446
  833.4 91.3 %reduce-scatter.29.cloned.1.call-done = f32[256,512]{1,0:T(8,128)} async-done(((f32[2048,512]{1,0:T(8,128)}), f32[256,512]{1,0:T(8,128)}) %reduce-scatter.29.cloned.1.call-update) | async-done | bytes 524304 | tf_op jit(solution)/shard_map/reduce_scatter | solution.py:446
  926.5 3.4 reverse_select_fusion.1
  936.9 3.4 reverse_select_fusion
  940.4 108.7 %all-reduce.9.cloned.1.call-done = f32[32,512]{1,0:T(8,128)} async-done(((f32[32,512]{1,0:T(8,128)}), f32[32,512]{1,0:T(8,128)}) %all-reduce.9.cloned.1.call-update) | async-done | bytes 65552 | tf_op jit(solution)/shard_map/psum | solution.py:448
  1051.9 45.1 %reduce-scatter.15.cloned.1.call-done = f32[2,256,512]{2,1,0:T(8,128)} async-done(((f32[2,1024,512]{2,1,0:T(8,128)}), f32[2,256,512]{2,1,0:T(8,128)}) %reduce-scatter.15.cloned.1.call-update) | async-done | bytes 1048592 | tf_op jit(solution)/shard_map/reduce_scatter | solution.py:438
  1099.0 53.2 %all-reduce.11.cloned.1.call-done = (f32[64,1536]{1,0:T(8,128)}, f32[64,512]{1,0:T(8,128)}, f32[64,512]{1,0:T(8,128)}, f32[64,1024]{1,0:T(8,128)}, f32[64,512]{1...) async-done(((f32[64,1536]{1,0:T(8,128)}, f32[64,512]{1,0:T(8,128)}, f32[64,512]{1,0:T(8,128)}, f32[64,1024]{1,0:T(8,128)}, f32[64,512]{1,0:T(8,128)}, ...) | async-done | bytes 2097168 | tf_op jit(solution)/shard_map/psum | solution.py:446
  1161.7 51.6 %reduce-scatter.11.cloned.1.call-done = f32[2,384,512]{2,1,0:T(8,128)} async-done(((f32[2,1536,512]{2,1,0:T(8,128)}), f32[2,384,512]{2,1,0:T(8,128)}) %reduce-scatter.11.cloned.1.call-update) | async-done | bytes 1572880 | tf_op jit(solution)/shard_map/reduce_scatter | solution.py:438
  1215.7 58.5 %reduce-scatter.13.cloned.1.call-done = f32[2,384,512]{2,1,0:T(8,128)} async-done(((f32[2,1536,512]{2,1,0:T(8,128)}), f32[2,384,512]{2,1,0:T(8,128)}) %reduce-scatter.13.cloned.1.call-update) | async-done | bytes 1572880 | tf_op jit(solution)/shard_map/reduce_scatter | solution.py:438
  (135 shorter events, 59.8 us)
Async XLA Ops:
  7.2 54.6 %copy-start.15 = (bf16[64,512]{1,0:T(8,128)(2,1)S(1)}, bf16[64,512]{1,0:T(8,128)(2,1)}, u32[]{:S(2)}) copy-start(bf16[64,512]{1,0:T(8,128)(2,1)} %param.22) | copy-start | bytes 196612
  7.2 88.3 %copy-start.16 = (bf16[64,512]{1,0:T(8,128)(2,1)S(1)}, bf16[64,512]{1,0:T(8,128)(2,1)}, u32[]{:S(2)}) copy-start(bf16[64,512]{1,0:T(8,128)(2,1)} %param.23) | copy-start | bytes 196612
  7.2 122.3 %copy-start.17 = (bf16[64,512]{1,0:T(8,128)(2,1)S(1)}, bf16[64,512]{1,0:T(8,128)(2,1)}, u32[]{:S(2)}) copy-start(bf16[64,512]{1,0:T(8,128)(2,1)} %param.25) | copy-start | bytes 196612
  7.2 155.9 %all-gather.21.cloned.1.call-start = ((), (), s32[]{:S(2)}) async-start(), calls=%async_computation.26 | async-start | bytes 2621440 | tf_op jit(solution)/shard_map/all_gather | solution.py:404
  7.9 157.4 %all-gather.23.cloned.1.call-start = ((), (), s32[]{:S(2)}) async-start(), calls=%async_computation.27 | async-start | bytes 3932160 | tf_op jit(solution)/shard_map/all_gather | solution.py:404
  8.7 159.3 %all-gather.19.cloned.1.call-start = ((), (), s32[]{:S(2)}) async-start(), calls=%async_computation.25 | async-start | bytes 3932160 | tf_op jit(solution)/shard_map/all_gather | solution.py:404
  9.4 161.3 %all-gather.13.cloned.1.call-start = ((), (), s32[]{:S(2)}) async-start(), calls=%async_computation.11 | async-start | bytes 1179648 | tf_op jit(solution)/shard_map/all_gather | solution.py:406
  10.0 175.1 %all-gather.11.cloned.1.call-start = ((), (), s32[]{:S(2)}) async-start(), calls=%async_computation.10 | async-start | bytes 1769472 | tf_op jit(solution)/shard_map/all_gather | solution.py:406
  10.6 224.6 %all-gather.15.cloned.1.call-start = ((), (), s32[]{:S(2)}) async-start(), calls=%async_computation.12 | async-start | bytes 2359296 | tf_op jit(solution)/shard_map/all_gather | solution.py:406
  11.2 274.0 %all-gather.17.cloned.1.call-start = ((), (), s32[]{:S(2)}) async-start(), calls=%async_computation.13 | async-start | bytes 2359296 | tf_op jit(solution)/shard_map/all_gather | solution.py:406
  11.9 450.2 %reduce-scatter.19.cloned.1.call-start = ((), (), s32[]{:S(2)}) async-start(), calls=%async_computation.18 | async-start | bytes 1179648 | tf_op jit(solution)/shard_map/reduce_scatter | solution.py:446
  373.4 3.3 copy-start.12
  373.4 3.3 copy-start.13
  373.4 5.0 copy-start.10
  373.4 5.0 copy-start.11
  376.6 151.8 %reduce-scatter.21.cloned.1.call-start = ((), (), s32[]{:S(2)}) async-start(), calls=%async_computation.19 | async-start | bytes 1179648 | tf_op jit(solution)/shard_map/reduce_scatter | solution.py:446
  378.3 215.9 %reduce-scatter.25.cloned.1.call-start = ((), (), s32[]{:S(2)}) async-start(), calls=%async_computation.21 | async-start | bytes 1179648 | tf_op jit(solution)/shard_map/reduce_scatter | solution.py:446
  380.0 3.2 copy-start.1
  380.0 285.1 %reduce-scatter.23.cloned.1.call-start = ((), (), s32[]{:S(2)}) async-start(), calls=%async_computation.20 | async-start | bytes 2359296 | tf_op jit(solution)/shard_map/reduce_scatter | solution.py:446
  383.1 2.7 copy-start.4
  385.8 356.4 %reduce-scatter.17.cloned.1.call-start = ((), (), s32[]{:S(2)}) async-start(), calls=%async_computation.17 | async-start | bytes 3538944 | tf_op jit(solution)/shard_map/reduce_scatter | solution.py:446
  389.1 3.4 copy-start.2
  389.1 2.7 copy-start.9
  396.2 437.2 %reduce-scatter.27.cloned.1.call-start = ((), (), s32[]{:S(2)}) async-start(), calls=%async_computation.22 | async-start | bytes 4718592 | tf_op jit(solution)/shard_map/reduce_scatter | solution.py:446
  403.0 521.7 %reduce-scatter.29.cloned.1.call-start = ((), (), s32[]{:S(2)}) async-start(), calls=%async_computation.23 | async-start | bytes 4718592 | tf_op jit(solution)/shard_map/reduce_scatter | solution.py:446
  410.0 639.1 %all-reduce.9.cloned.1.call-start = ((), (), s32[]{:S(2)}) async-start(), calls=%async_computation.24 | async-start | bytes 131072 | tf_op jit(solution)/shard_map/psum | solution.py:448
  410.5 686.4 %reduce-scatter.15.cloned.1.call-start = ((), (), s32[]{:S(2)}) async-start(), calls=%async_computation.16 | async-start | bytes 5242880 | tf_op jit(solution)/shard_map/reduce_scatter | solution.py:438
  416.1 736.1 %all-reduce.11.cloned.1.call-start = ((), (), s32[]{:S(2)}) async-start(), calls=%async_computation.28 | async-start | bytes 4194304 | tf_op jit(solution)/shard_map/psum | solution.py:446
  924.8 288.5 %reduce-scatter.11.cloned.1.call-start = ((), (), s32[]{:S(2)}) async-start(), calls=%async_computation.14 | async-start | bytes 7864320 | tf_op jit(solution)/shard_map/reduce_scatter | solution.py:438
  929.9 344.3 %reduce-scatter.13.cloned.1.call-start = ((), (), s32[]{:S(2)}) async-start(), calls=%async_computation.15 | async-start | bytes 7864320 | tf_op jit(solution)/shard_map/reduce_scatter | solution.py:438
  932.0 2.3 copy-start.6
  1152.2 8.7 copy-start.14
  (6 other events, 10.5 us)
Sparse Core Ops, SparseCore 0:
  9.6 25.2 all-gather.20
  36.5 28.6 all-gather.22
  66.7 28.5 all-gather.18
  97.3 42.6 all-gather.12
  142.0 43.0 all-gather.10
  187.1 48.0 all-gather.14
  237.4 47.7 all-gather.16
  376.7 85.3 reduce-scatter.18
  465.9 62.3 reduce-scatter.20
  531.6 62.5 reduce-scatter.24
  598.1 66.9 reduce-scatter.22
  668.9 73.2 reduce-scatter.16
  746.3 87.1 reduce-scatter.26
  836.9 87.7 reduce-scatter.28
  931.7 117.3 all-reduce.8
  1051.6 45.2 reduce-scatter.14
  1099.6 52.5 all-reduce.10
  1154.7 58.5 reduce-scatter.10
  1215.8 58.3 reduce-scatter.12

commit v2 on v1

--- a/solution.py
+++ b/solution.py
@@ -57,34 +57,36 @@
 
 def layer_kernel(
     bounds,
-    x_hbm, m_hbm, ct_ref, vec_ref,
-    wqkv_hbm, wout_hbm, wcq_hbm, wckv_hbm, wcout_hbm, wup_hbm, wdown_hbm,
+    x_hbm, m_hbm, x_ref, ct_ref, vec_all, w_hbm, wdown_hbm,
     layer_out, mixed_out, self_low_out, first_low_out, cdq_out, cmixed_out, cross_low_out,
     second_low_out, up_low_out, active_out, down_low_out, dq_out, part_out,
     dkv_hbm, dckv_hbm, vecg_out,
     wqkv, wout, wcq, wckv, wcout, wup, wdown,
-    xs, ms, k_s, kt_s, v_s, vt_s, k_c, kt_c, v_c, vt_c,
+    k_s, kt_s, v_s, vt_s, k_c, kt_c, v_c, vt_c,
     p_s, p_c, dk_s, dv_s, dk_c, dv_c,
-    qm_s, qm_c, gtm, gm, ot_s, ot_c, dqt, slope_s, sems,
+    qm_s, qm_c, gtm, gm, ot_s, ot_c, dqt, slope_s, vec_ref, sems,
 ):
     step = pl.program_id(0)
     steps = pl.num_programs(0)
-    d_model = xs.shape[1]
-    t_len = xs.shape[0]
-    s_len = ms.shape[0]
+    t_len, d_model = k_s.shape
+    s_len = k_c.shape[0]
     ff = wup.shape[1]
     hd = d_model // H
     core = bounds[0]
     block = 2 * step + core
 
+    def columns(start, count):
+        return w_hbm.at[:, pl.ds(start * d_model, count * d_model)]
+
     loads = [
         pltpu.make_async_copy(src, dst, sems.at[n])
         for n, (src, dst) in enumerate((
-            (x_hbm, xs), (wqkv_hbm, wqkv), (m_hbm, ms), (wckv_hbm, wckv), (wout_hbm, wout), (wcq_hbm, wcq),
-            (wcout_hbm, wcout), (wup_hbm, wup), (wdown_hbm, wdown),
+            (columns(0, 3), wqkv), (x_hbm.at[:, pl.ds(0, 256)], p_s.at[0]), (x_hbm.at[:, pl.ds(256, 256)], p_s.at[1]),
+            (columns(5, 2), wckv), (m_hbm.at[:, pl.ds(0, 256)], p_c.at[0]), (m_hbm.at[:, pl.ds(256, 256)], p_c.at[1]),
+            (columns(3, 1), wout), (columns(4, 1), wcq), (columns(7, 1), wcout), (columns(8, ff // d_model), wup),
+            (wdown_hbm, wdown),
         ))
     ]
-    vec = vec_ref[...]
 
     @pl.when(step == 0)
     def _():
@@ -95,6 +97,8 @@
         dk_c[...] = jnp.zeros_like(dk_c)
         dv_c[...] = jnp.zeros_like(dv_c)
         vecg_out[...] = jnp.zeros_like(vecg_out)
+        vec_ref[...] = jnp.sum(vec_all[...].astype(F32), axis=0)
+        vec = vec_ref[...]
         vec_t = vec.T
 
         def project(rows_ref, w_ref, k_at, kt, k, vt, v, bias_row, bias_row_t, count):
@@ -105,7 +109,7 @@
 
             def one(r, carry):
                 at = pl.ds(pl.multiple_of(r * RB, RB), RB)
-                rows = rows_ref[at, :]
+                rows = jnp.concatenate([rows_ref[0, at, :], rows_ref[1, at, :]], axis=1)
                 k[at, :] = mm(rows, wk).astype(BF16)
                 v[at, :] = (mm(rows, wv) + bias_row).astype(BF16)
                 kt[:, at] = mm_nt(wk_t, rows).astype(BF16)
@@ -114,14 +118,16 @@
 
             lax.fori_loop(0, count // RB, one, 0)
 
-        loads[0].wait()
-        loads[1].wait()
-        project(xs, wqkv, d_model, kt_s, k_s, vt_s, v_s, vec[1:2], vec_t[:, 1:2], t_len)
-        loads[2].wait()
-        loads[3].wait()
-        project(ms, wckv, 0, kt_c, k_c, vt_c, v_c, vec[4:5], vec_t[:, 4:5], s_len)
-        for load in loads[4:]:
+        for load in loads[:3]:
             load.wait()
+        project(p_s, wqkv, d_model, kt_s, k_s, vt_s, v_s, vec[1:2], vec_t[:, 1:2], t_len)
+        for load in loads[3:6]:
+            load.wait()
+        project(p_c, wckv, 0, kt_c, k_c, vt_c, v_c, vec[4:5], vec_t[:, 4:5], s_len)
+        for load in loads[6:]:
+            load.wait()
+
+    vec = vec_ref[...]
 
     qpos = block * RB + lax.broadcasted_iota(jnp.int32, (1, RB), 1)
     lo_s = jnp.zeros((1, RB), jnp.int32)
@@ -182,13 +188,17 @@
             at = pl.ds(pl.multiple_of(j * KB, KB), KB)
             bias = bias_of(j)
             out = []
+            sc = [scores(h, at, bias) for h in range(H)]
+            lows = []
             for h in range(H):
-                weights = jnp.exp(scores(h, at, bias) - highest[h])
+                weights = jnp.exp(sc[h] - highest[h])
                 low = weights.astype(BF16)
+                lows.append(low)
                 p[h, at, :] = low
                 out.append(totals[h] + fold(weights, jnp.sum))
+            for h in range(H):
                 head = slice(h * hd, (h + 1) * hd)
-                ot[head, :] += mm(vt[head, at], low)
+                ot[head, :] += mm(vt[head, at], lows[h])
             return tuple(out)
 
         totals = lax.fori_loop(j_from, j_to, gather, tuple(jnp.zeros((8, RB), F32) for _ in range(H)))
@@ -216,22 +226,16 @@
 
         def body(j, carry):
             at = pl.ds(pl.multiple_of(j * KB, KB), KB)
-            for pair_index in range(H // 2):
-                pair = slice(pair_index * 2 * hd, (pair_index + 1) * 2 * hd)
-                dk_part = None
-                dv_part = None
-                for h in (2 * pair_index, 2 * pair_index + 1):
-                    low = p[h, at, :]
-                    prob_grad = mm(v[at, pair], gtm[h])
-                    score_low = (low.astype(F32) * (prob_grad - spread[h])).astype(BF16)
-                    dv_h = mm(low, gm[h])
-                    dk_h = mm(score_low, qm[h])
-                    dv_part = dv_h if dv_part is None else dv_part + dv_h
-                    dk_part = dk_h if dk_part is None else dk_part + dk_h
-                    head = slice(h * hd, (h + 1) * hd)
-                    dqt[head, :] += mm(kt[head, at], score_low)
-                dk[at, pair] += dk_part
-                dv[at, pair] += dv_part
+            pairs = [slice((h // 2) * 2 * hd, (h // 2 + 1) * 2 * hd) for h in range(H)]
+            prob_grads = [mm(v[at, pairs[h]], gtm[h]) for h in range(H)]
+            for h in range(0, H, 2):
+                dv[at, pairs[h]] += mm(p[h, at, :], gm[h]) + mm(p[h + 1, at, :], gm[h + 1])
+            lows = [(p[h, at, :].astype(F32) * (prob_grads[h] - spread[h])).astype(BF16) for h in range(H)]
+            for h in range(0, H, 2):
+                dk[at, pairs[h]] += mm(lows[h], qm[h]) + mm(lows[h + 1], qm[h + 1])
+            for h in range(H):
+                head = slice(h * hd, (h + 1) * hd)
+                dqt[head, :] += mm(kt[head, at], lows[h])
             return carry
 
         lax.fori_loop(j_from, j_to, body, 0)
@@ -240,7 +244,7 @@
     def add_vec(row, values):
         vecg_out[row:row + 1, :] += jnp.sum(values, axis=0, keepdims=True)
 
-    x_rows = xs[pl.ds(pl.multiple_of(first, RB), RB), :]
+    x_rows = x_ref[...]
     q = ((mm(x_rows, wqkv[:, :d_model]) + vec[0:1]) * 0.125).astype(BF16)
     put_masked(q, q.T, qm_s, gtm)
     inv_s = attend(gtm, k_s, vt_s, p_s, ot_s, lo_s, hi_s, s_from, s_to)
@@ -330,10 +334,10 @@
             store.wait()
 
 
-def run_layer(bounds, x_full, m_full, ct_full, vec, weights):
+def run_layer(bounds, x_full, m_full, ct_full, vec_all, w_all, w_down):
     t_len, d_model = x_full.shape
     s_len = m_full.shape[0]
-    ff = weights[5].shape[1]
+    ff = w_down.shape[0]
     steps = t_len // (2 * RB)
     own = t_len // 2
     any_spec = pl.BlockSpec(memory_space=pl.ANY)
@@ -354,15 +358,14 @@
     out_specs += [any_spec, any_spec, pl.BlockSpec((32, d_model), lambda i, b: (0, 0))]
     bf = lambda *shape: pltpu.VMEM(shape, BF16)
     fl = lambda *shape: pltpu.VMEM(shape, F32)
-    scratch = [bf(*w.shape) for w in weights] + [
-        bf(t_len, d_model), bf(s_len, d_model),
+    scratch = [bf(d_model, n * d_model) for n in (3, 1, 1, 2, 1)] + [bf(d_model, ff), bf(ff, d_model)] + [
         bf(t_len, d_model), bf(d_model, t_len), bf(t_len, d_model), bf(d_model, t_len),
         bf(s_len, d_model), bf(d_model, s_len), bf(s_len, d_model), bf(d_model, s_len),
         bf(H, t_len, RB), bf(H, s_len, RB),
         fl(t_len, d_model), fl(t_len, d_model), fl(s_len, d_model), fl(s_len, d_model),
         bf(H, RB, 128), bf(H, RB, 128), bf(H, 128, RB), bf(H, RB, 128),
-        fl(d_model, RB), fl(d_model, RB), fl(d_model, RB), fl(RB, ff),
-        pltpu.SemaphoreType.DMA((9,)),
+        fl(d_model, RB), fl(d_model, RB), fl(d_model, RB), fl(RB, ff), fl(32, d_model),
+        pltpu.SemaphoreType.DMA((11,)),
     ]
     return pl.pallas_call(
         layer_kernel,
@@ -370,14 +373,591 @@
         grid_spec=pltpu.PrefetchScalarGridSpec(
             num_scalar_prefetch=1,
             grid=(steps,),
-            in_specs=[any_spec, any_spec, pl.BlockSpec((RB, d_model), lambda i, b: (2 * i + b[0], 0)),
-                      pl.BlockSpec((32, d_model), lambda i, b: (0, 0))] + [any_spec] * 7,
+            in_specs=[any_spec, any_spec] + [pl.BlockSpec((RB, d_model), lambda i, b: (2 * i + b[0], 0))] * 2 + [
+                      pl.BlockSpec(vec_all.shape, lambda i, b: (0, 0, 0)), any_spec, any_spec],
             out_specs=out_specs,
             scratch_shapes=scratch,
         ),
         compiler_params=pltpu.CompilerParams(vmem_limit_bytes=64 * 1024 * 1024 - 512 * 1024),
         name="layer",
-    )(bounds, x_full, m_full, ct_full, vec, *weights)
+    )(bounds, x_full, m_full, x_full, ct_full, vec_all, w_all, w_down)
+
+
+def ring_neighbours(at, size):
+    odd = lax.rem(at, 2)
+    after = jnp.where(odd == 0, jnp.where(at + 2 < size, at + 2, at + 1), jnp.where(at >= 3, at - 2, at - 1))
+    before = jnp.where(odd == 0, jnp.where(at >= 2, at - 2, at + 1), jnp.where(at + 2 < size, at + 2, at - 1))
+    return after, before
+
+
+def ring_place(at, size):
+    return jnp.where(lax.rem(at, 2) == 0, lax.div(at, 2), size - 1 - lax.div(at, 2))
+
+
+def ring_member(place, size):
+    place = lax.rem(place + 2 * size, size)
+    return jnp.where(place < lax.div(size, 2), 2 * place, 2 * (size - 1 - place) + 1)
+
+
+def gather_kernel(
+    size, splits,
+    tokens, memory, cotangent, counts, packed, w_qkv, w_out, w_cq, w_ckv, w_cout, w_up, w_down,
+    x_full, m_full, c_full, counts_all, vec_all, w_all, d_all,
+    send_ring, recv_ring, send_core, recv_core, local_sems, send_rows, recv_rows,
+):
+    at, place = lax.axis_index("dp"), lax.axis_index("seq")
+    micro, core = lax.div(place, 2), lax.rem(place, 2)
+    after, before = ring_neighbours(at, size)
+    mine = ring_place(at, size)
+    core_peer = {"seq": place + 1 - 2 * core}
+    chip_peer = {"seq": place + 2 - 4 * micro}
+    peers = ({"dp": after}, {"dp": before}, core_peer, chip_peer)
+
+    barrier = pltpu.get_barrier_semaphore()
+    for peer in peers:
+        pl.semaphore_signal(barrier, inc=1, device_id=peer, device_id_type=pl.DeviceIdType.MESH)
+
+    wide, tall = w_qkv.shape[0], w_down.shape[0]
+    local = []
+    for n, (shard, column) in enumerate(zip((w_qkv, w_out, w_cq, w_ckv, w_cout, w_up), splits)):
+        local.append(pltpu.make_async_copy(
+            shard, w_all.at[pl.ds(at * wide, wide), pl.ds(column, shard.shape[1])], local_sems.at[n]))
+    local.append(pltpu.make_async_copy(w_down, d_all.at[pl.ds(at * tall, tall)], local_sems.at[6]))
+    local.append(pltpu.make_async_copy(packed, vec_all.at[at], local_sems.at[7]))
+    for copy in local:
+        copy.start()
+
+    pairs = ((tokens, x_full), (memory, m_full), (cotangent, c_full), (counts, counts_all))
+
+    def chunk(n, owner):
+        source, full = pairs[n]
+        rows = source.shape[-2]
+        return full.at[pl.ds(owner * rows, rows)]
+
+    def rows_of(n, index):
+        source = pairs[n][0]
+        return source.at[index, 0]
+
+    pl.semaphore_wait(barrier, 4)
+    across, near, own = [], [], []
+    for n in range(4):
+        copy = pltpu.make_async_remote_copy(
+            rows_of(n, 1 - micro), chunk(n, place), send_rows.at[n, 0], recv_rows.at[n, 0],
+            device_id=chip_peer, device_id_type=pl.DeviceIdType.MESH)
+        copy.start()
+        across.append(copy)
+    for n in range(4):
+        copy = pltpu.make_async_remote_copy(
+            rows_of(n, micro), chunk(n, place), send_rows.at[n, 1], recv_rows.at[n, 1],
+            device_id=core_peer, device_id_type=pl.DeviceIdType.MESH)
+        copy.start()
+        near.append(copy)
+        copy = pltpu.make_async_copy(rows_of(n, micro), chunk(n, place), local_sems.at[8 + n])
+        copy.start()
+        own.append(copy)
+    for copy in local:
+        copy.wait()
+
+    def piece(stream, way, owner):
+        if stream == 2:
+            return vec_all.at[owner, pl.ds(16 * way, 16)]
+        full, rows = ((w_all, wide), (d_all, tall))[stream]
+        quarter = rows // 4
+        return full.at[pl.ds(owner * rows + (2 * core + way) * quarter, quarter)]
+
+    ring_sends, core_copies = [], []
+
+    def ring_send(stream, way, step, owner):
+        copy = pltpu.make_async_remote_copy(
+            piece(stream, way, owner), piece(stream, way, owner), send_ring.at[stream, way, step],
+            recv_ring.at[stream, way, step], device_id={"dp": after if way == 0 else before},
+            device_id_type=pl.DeviceIdType.MESH)
+        copy.start()
+        ring_sends.append(copy)
+        return copy
+
+    current = {}
+    for stream in (2, 0, 1):
+        for way in range(2):
+            current[stream, way] = ring_send(stream, way, 0, at)
+    for step in range(1, size):
+        for stream in (2, 0, 1):
+            for way in range(2):
+                owner = ring_member(mine - step if way == 0 else mine + step, size)
+                current[stream, way].wait_recv()
+                if step < size - 1:
+                    current[stream, way] = ring_send(stream, way, step, owner)
+                if stream < 2:
+                    copy = pltpu.make_async_remote_copy(
+                        piece(stream, way, owner), piece(stream, way, owner), send_core.at[stream, way, step - 1],
+                        recv_core.at[stream, way, step - 1], device_id=core_peer,
+                        device_id_type=pl.DeviceIdType.MESH)
+                    copy.start()
+                    core_copies.append(copy)
+        if step <= 4:
+            n = step - 1
+            across[n].wait_recv()
+            other = chunk(n, place + 2 - 4 * micro)
+            copy = pltpu.make_async_remote_copy(
+                other, other, send_rows.at[n, 2], recv_rows.at[n, 2],
+                device_id=core_peer, device_id_type=pl.DeviceIdType.MESH)
+            copy.start()
+            core_copies.append(copy)
+    for copy in own:
+        copy.wait()
+    for copy in near + core_copies:
+        copy.wait()
+    for copy in across + ring_sends:
+        copy.wait_send()
+
+
+def gather_fused(tokens, memory, cotangent, counts, packed, shards):
+    size = lax.axis_size("dp")
+    d_model = tokens.shape[3]
+    widths = [shard.shape[1] for shard in shards[:6]]
+    splits = [sum(widths[:n]) for n in range(6)]
+    seq = lax.axis_size("seq")
+    any_spec = pl.BlockSpec(memory_space=pl.ANY)
+    out_shape = [jax.ShapeDtypeStruct((seq * a.shape[2], d_model), BF16) for a in (tokens, memory, cotangent)]
+    out_shape += [
+        jax.ShapeDtypeStruct((seq * 8, 128), jnp.int32),
+        jax.ShapeDtypeStruct((size, 32, d_model), BF16),
+        jax.ShapeDtypeStruct((size * shards[0].shape[0], sum(widths)), BF16),
+        jax.ShapeDtypeStruct((size * shards[6].shape[0], d_model), BF16),
+    ]
+    dma = pltpu.SemaphoreType.DMA
+    return pl.pallas_call(
+        functools.partial(gather_kernel, size, splits),
+        out_shape=out_shape,
+        in_specs=[pl.BlockSpec(memory_space=pltpu.VMEM)] * 12,
+        out_specs=[any_spec] * 7,
+        scratch_shapes=[dma((3, 2, size)), dma((3, 2, size)), dma((2, 2, size)), dma((2, 2, size)), dma((12,)),
+                        dma((4, 3)), dma((4, 3))],
+        compiler_params=pltpu.CompilerParams(collective_id=0, has_side_effects=True),
+        name="gather",
+    )(tokens, memory, cotangent, counts, packed, *shards)
+
+
+MESH = pl.DeviceIdType.MESH
+STREAMS = ("down", "up", "qkv", "pair", "outs")
+
+
+def stream_shapes(d_model, ff, size):
+    quarters = (d_model // 4, ff // 4, 3 * d_model // 4, 2 * d_model // 4, 3 * d_model // 4)
+    rows = (ff, d_model, d_model, d_model, d_model)
+    return [(r, r // size, q) for r, q in zip(rows, quarters)]
+
+
+def settle_kernel(size, shapes, *refs):
+    n_in, n_out, count = 18, 4 + 2 * len(shapes), len(shapes)
+    (x_hbm, m_hbm, w_hbm, lo_hbm, mixed_hbm, self_low_hbm, first_low_hbm, cdq_hbm, cmixed_hbm, cross_low_hbm,
+     second_low_hbm, up_low_hbm, active_hbm, down_low_hbm, dq_hbm, part_hbm, dkv_hbm, dckv_hbm) = refs[:n_in]
+    vec_hbm = refs[n_in]
+    outs = refs[n_in + 1:n_in + 1 + n_out]
+    lo_home, dt_home, dm_home, vec_out = outs[:4]
+    ga, gb = outs[4:4 + count], outs[4 + count:]
+    scratch = refs[n_in + 1 + n_out:]
+    (xf, mf, wkv, wpair, xo, mixed, self_low, first_low, cdq, cmixed, cross_low, second_low, up_low, active,
+     down_low, dq, part, dkv, dckv) = scratch[:19]
+    (tz, tz_low, tz_got, mz, mz_low, mz_got, lo_buf, vec_run, vec_got) = scratch[19:28]
+    rest = scratch[28:]
+    acc, stage, other, ring_out, ring_in, fin = (rest[n * count:(n + 1) * count] for n in range(6))
+    (load_sems, store_sems, ring_ss, ring_rs, core_ss, core_rs, fin_ss, fin_rs, row_ss, row_rs, vec_ss, vec_rs,
+     lo_ss, lo_rs) = rest[6 * count:]
+
+    at, place = lax.axis_index("dp"), lax.axis_index("seq")
+    micro, core = lax.div(place, 2), lax.rem(place, 2)
+    after, before = ring_neighbours(at, size)
+    mine = ring_place(at, size)
+    core_peer = {"seq": place + 1 - 2 * core}
+    chip_peer = {"seq": place + 2 - 4 * micro}
+    levels = size.bit_length() - 1
+    flips = [{"dp": at + (1 << n) * (1 - 2 * lax.rem(lax.div(at, 1 << n), 2))} for n in range(levels)]
+    vec_peers = [core_peer, chip_peer] + flips
+    d_model = xf.shape[1]
+    half = d_model // 2
+    t_len, s_len = xf.shape[0], mf.shape[0]
+
+    barrier = pltpu.get_barrier_semaphore()
+    greeted = [{"dp": after}, {"dp": before}, core_peer, chip_peer] + flips
+    for peer in greeted:
+        pl.semaphore_signal(barrier, inc=1, device_id=peer, device_id_type=MESH)
+
+    loads = {}
+
+    def load(name, src, dst):
+        copy = pltpu.make_async_copy(src, dst, load_sems.at[len(loads)])
+        copy.start()
+        loads[name] = copy
+
+    load("vec", vec_hbm.at[pl.ds(0, 24)], vec_run.at[0])
+    load("active", active_hbm, active)
+    load("down_low", down_low_hbm, down_low)
+    load("second_low", second_low_hbm, second_low)
+    load("up_low", up_low_hbm, up_low)
+    load("dkv", dkv_hbm, dkv)
+    load("wkv", w_hbm.at[:, pl.ds(d_model, 2 * d_model)], wkv)
+    load("part", part_hbm, part)
+    load("dckv", dckv_hbm, dckv)
+    load("wpair", w_hbm.at[:, pl.ds(5 * d_model, 2 * d_model)], wpair)
+    load("xf", x_hbm, xf)
+    for n in range(t_len // (2 * RB)):
+        load(("xo", n), x_hbm.at[pl.ds((2 * n + core) * RB, RB)], xo.at[pl.ds(n * RB, RB)])
+    load("dq", dq_hbm, dq)
+    load("mf", m_hbm, mf)
+    for name, src, dst in (("mixed", mixed_hbm, mixed), ("self_low", self_low_hbm, self_low),
+                           ("first_low", first_low_hbm, first_low), ("cdq", cdq_hbm, cdq),
+                           ("cmixed", cmixed_hbm, cmixed), ("cross_low", cross_low_hbm, cross_low)):
+        load(name, src, dst)
+
+    pending = []
+
+    def send(src, dst, send_sem, recv_sem, peer):
+        copy = pltpu.make_async_remote_copy(src, dst, send_sem, recv_sem, device_id=peer, device_id_type=MESH)
+        copy.start()
+        pending.append(copy)
+        return copy
+
+    stores = []
+
+    def store(src, dst):
+        copy = pltpu.make_async_copy(src, dst, store_sems.at[len(stores)])
+        copy.start()
+        stores.append(copy)
+
+    pl.semaphore_wait(barrier, len(greeted))
+
+    piece = t_len // 12
+    keep, give = [], []
+
+    def pieces_of(index0, slot0, index1, slot1):
+        index, slot = jnp.where(core == 0, index0, index1), jnp.where(core == 0, slot0, slot1)
+        source = lo_hbm.at[pl.ds(pl.multiple_of(index * piece, 128), piece)]
+        return source, lo_buf.at[lax.div(slot, 3), pl.ds(pl.multiple_of(lax.rem(slot, 3) * piece, 128), piece)]
+
+    for n, row in enumerate(((0, 0, 1, 0), (1, 1, 4, 4), (4, 5, 5, 5))):
+        copy = pltpu.make_async_copy(*pieces_of(*row), lo_ss.at[n])
+        copy.start()
+        keep.append(copy)
+    for n, row in enumerate(((2, 1, 0, 2), (3, 2, 2, 3), (5, 3, 3, 4))):
+        source, target = pieces_of(*row)
+        give.append(send(source, target, lo_ss.at[3 + n], lo_rs.at[n], core_peer))
+
+    vec_state = {"level": 0, "copy": None}
+
+    def vec_send():
+        level = vec_state["level"]
+        vec_state["copy"] = send(vec_run.at[level], vec_got.at[level], vec_ss.at[level], vec_rs.at[level],
+                                 vec_peers[level])
+
+    def vec_step():
+        level = vec_state["level"]
+        vec_state["copy"].wait_recv()
+        vec_run[level + 1] = vec_run[level] + vec_got[level]
+        vec_state["level"] = level + 1
+        if level + 1 < len(vec_peers):
+            vec_send()
+        else:
+            store(vec_run.at[level + 1], vec_out)
+
+    loads["vec"].wait()
+    vec_send()
+
+    row_waits = []
+
+    def home_rows(n, rows_of, home):
+        store(rows_of(micro), home.at[micro])
+        row_waits.append(send(rows_of(1 - micro), home.at[micro], row_ss.at[n], row_rs.at[n], chip_peer))
+
+    def split(values, pieces, s, rows):
+        width = values.shape[1] // pieces
+        quarter = width // 4
+        for p in range(pieces):
+            lower = values[:, p * width:p * width + 2 * quarter]
+            upper = values[:, p * width + 2 * quarter:(p + 1) * width]
+            own = jnp.where(core == 0, lower, upper)
+            away = jnp.where(core == 0, upper, lower).astype(BF16)
+            for way in range(2):
+                acc[s][way, rows, p * quarter:(p + 1) * quarter] = own[:, way * quarter:(way + 1) * quarter]
+                stage[s][way, rows, p * quarter:(p + 1) * quarter] = away[:, way * quarter:(way + 1) * quarter]
+
+    core_waits = {}
+
+    def compute(s):
+        tile = 256
+        if s == 0:
+            loads["active"].wait()
+            loads["down_low"].wait()
+
+            def one(m, carry):
+                rows = pl.ds(pl.multiple_of(m * tile, tile), tile)
+                split(mm_tn(active[:, rows], down_low[...]), 1, s, rows)
+                return carry
+
+            lax.fori_loop(0, active.shape[1] // tile, one, 0)
+        elif s == 1:
+            loads["second_low"].wait()
+            loads["up_low"].wait()
+
+            def one(m, carry):
+                rows = pl.ds(pl.multiple_of(m * tile, tile), tile)
+                split(mm_tn(second_low[:, rows], up_low[...]), 1, s, rows)
+                return carry
+
+            lax.fori_loop(0, d_model // tile, one, 0)
+        elif s == 2:
+            loads["xf"].wait()
+            for n in range(t_len // (2 * RB)):
+                loads["xo", n].wait()
+            loads["dq"].wait()
+
+            def one(m, carry):
+                rows = pl.ds(pl.multiple_of(m * tile, tile), tile)
+                parts = [mm_tn(xo[:, rows], dq[...])]
+                whole = xf[:, rows]
+                parts += [mm_tn(whole, dkv[n]) for n in range(4)]
+                split(jnp.concatenate(parts, axis=1), 3, s, rows)
+                return carry
+
+            lax.fori_loop(0, d_model // tile, one, 0)
+        elif s == 3:
+            loads["mf"].wait()
+
+            def one(m, carry):
+                rows = pl.ds(pl.multiple_of(m * tile, tile), tile)
+                whole = mf[:, rows]
+                split(jnp.concatenate([mm_tn(whole, dckv[n]) for n in range(4)], axis=1), 2, s, rows)
+                return carry
+
+            lax.fori_loop(0, d_model // tile, one, 0)
+        else:
+            for name in ("mixed", "self_low", "first_low", "cdq", "cmixed", "cross_low"):
+                loads[name].wait()
+
+            def one(m, carry):
+                rows = pl.ds(pl.multiple_of(m * tile, tile), tile)
+                parts = [mm_tn(mixed[:, rows], self_low[...]), mm_tn(first_low[:, rows], cdq[...]),
+                         mm_tn(cmixed[:, rows], cross_low[...])]
+                split(jnp.concatenate(parts, axis=1), 3, s, rows)
+                return carry
+
+            lax.fori_loop(0, d_model // tile, one, 0)
+        core_waits[s] = send(stage[s], other[s], core_ss.at[s], core_rs.at[s], core_peer)
+
+    ring_waits = {}
+
+    def ring(s, step):
+        block = shapes[s][1]
+        if step == 0:
+            core_waits[s].wait_recv()
+        for way in range(2):
+            owner = ring_member(mine - 1 - step if way == 0 else mine + 1 + step, size)
+            rows = pl.ds(owner * block, block)
+            total = acc[s][way, rows, :] + other[s][way, rows, :].astype(F32)
+            if step > 0:
+                ring_waits[s, way].wait_recv()
+                total = total + ring_in[s][way, step - 1].astype(F32)
+            if step < size - 1:
+                ring_out[s][way, step] = total.astype(BF16)
+                ring_waits[s, way] = send(
+                    ring_out[s].at[way, step], ring_in[s].at[way, step], ring_ss.at[s, way, step],
+                    ring_rs.at[s, way, step], {"dp": after if way == 0 else before})
+            else:
+                fin[s][way] = total.astype(BF16)
+
+    chip_waits, tail = {}, []
+
+    def finish(s):
+        store(fin[s], ga[s].at[core])
+        chip_waits[s] = send(fin[s], gb[s].at[core], fin_ss.at[s, 0], fin_rs.at[s, 0], chip_peer)
+        tail.append(send(fin[s], ga[s].at[core], fin_ss.at[s, 1], fin_rs.at[s, 1], core_peer))
+
+    def forward(s):
+        chip_waits[s].wait_recv()
+        tail.append(send(gb[s].at[core], gb[s].at[core], fin_ss.at[s, 2], fin_rs.at[s, 2], core_peer))
+
+    def row_products():
+        for name in ("dkv", "wkv", "part", "dckv", "wpair"):
+            loads[name].wait()
+
+        def tokens(b, carry):
+            rows = pl.ds(pl.multiple_of(b * RB, RB), RB)
+            total = None
+            for n in range(4):
+                product = mm_nt(dkv[n, rows, :], wkv[:, n * 256:(n + 1) * 256])
+                total = product if total is None else total + product
+            own = part[pl.ds(pl.multiple_of(lax.div(b, 2) * RB, RB), RB), :]
+            total = total + jnp.where(lax.rem(b, 2) == core, own, jnp.zeros_like(own))
+            tz[rows, :] = total
+            tz_low[rows, :] = total.astype(BF16)
+            return carry
+
+        lax.fori_loop(0, t_len // RB, tokens, 0)
+
+        def memories(b, carry):
+            rows = pl.ds(pl.multiple_of(b * RB, RB), RB)
+            total = None
+            for n in range(4):
+                product = mm_nt(dckv[n, rows, :], wpair[:, n * 256:(n + 1) * 256])
+                total = product if total is None else total + product
+            mz[rows, :] = total
+            mz_low[rows, :] = total.astype(BF16)
+            return carry
+
+        lax.fori_loop(0, s_len // RB, memories, 0)
+        copies = []
+        for n, (low, got, length) in enumerate(((tz_low, tz_got, t_len // 4), (mz_low, mz_got, s_len // 4))):
+            for k in range(2):
+                start = pl.multiple_of((1 - core + 2 * k) * length, 128)
+                copies.append(send(low.at[pl.ds(start, length)], got.at[k], row_ss.at[3 + 2 * n + k],
+                                   row_rs.at[3 + 2 * n + k], core_peer))
+        return copies
+
+    def row_finish(copies):
+        for copy in copies:
+            copy.wait_recv()
+        for n, (full, got, done, length, home) in enumerate((
+                (tz, tz_got, tz_low, t_len // 4, dt_home), (mz, mz_got, mz_low, s_len // 4, dm_home))):
+
+            def rows_at(k, length=length):
+                return pl.ds(pl.multiple_of((core + 2 * k) * length, 128), length)
+
+            for k in range(2):
+                done[rows_at(k), :] = (full[rows_at(k), :] + got[k].astype(F32)).astype(BF16)
+            home_rows(1 + n, lambda k, done=done, rows_at=rows_at: done.at[rows_at(k)], home)
+
+    compute(0)
+    ring(0, 0)
+    for copy in keep:
+        copy.wait()
+    for copy in give:
+        copy.wait_recv()
+    home_rows(0, lambda k: lo_buf.at[k], lo_home)
+    vec_step()
+    compute(1)
+    ring(1, 0)
+    ring(0, 1)
+    vec_step()
+    row_copies = row_products()
+    ring(0, 2)
+    row_finish(row_copies)
+    vec_step()
+    compute(2)
+    ring(2, 0)
+    ring(1, 1)
+    ring(0, 3)
+    vec_step()
+    compute(3)
+    ring(3, 0)
+    ring(2, 1)
+    ring(1, 2)
+    ring(0, 4)
+    vec_step()
+    compute(4)
+    ring(4, 0)
+    done = {0: 4, 1: 2, 2: 1, 3: 0, 4: 0}
+    while any(done[s] < size - 1 for s in range(count)):
+        for s in range(count - 1, -1, -1):
+            if done[s] < size - 1:
+                done[s] += 1
+                ring(s, done[s])
+                if done[s] == size - 1:
+                    finish(s)
+        while vec_state["level"] < len(vec_peers):
+            vec_step()
+    for s in range(count):
+        forward(s)
+    for copy in row_waits + tail:
+        copy.wait_recv()
+    for copy in pending:
+        copy.wait_send()
+    for copy in stores:
+        copy.wait()
+
+
+def settle_fused(x_full, m_full, w_all, results):
+    size = lax.axis_size("dp")
+    (layer_rows, mixed, self_low, first_low, cdq, cmixed, cross_low, second_low, up_low, active, down_low, dq,
+     part, dkv, dckv, vec_sums) = results
+    t_len, d_model = x_full.shape
+    s_len, ff, own = m_full.shape[0], up_low.shape[1], dq.shape[0]
+    shapes = stream_shapes(d_model, ff, size)
+    any_spec = pl.BlockSpec(memory_space=pl.ANY)
+    out_shape = [
+        jax.ShapeDtypeStruct((2, t_len // 4, d_model), BF16),
+        jax.ShapeDtypeStruct((2, t_len // 4, d_model), BF16),
+        jax.ShapeDtypeStruct((2, s_len // 4, d_model), BF16),
+        jax.ShapeDtypeStruct((24, d_model), F32),
+    ]
+    out_shape += [jax.ShapeDtypeStruct((2, 2, block, q), BF16) for _, block, q in shapes] * 2
+    bf = lambda *shape: pltpu.VMEM(shape, BF16)
+    fl = lambda *shape: pltpu.VMEM(shape, F32)
+    dma = pltpu.SemaphoreType.DMA
+    levels = 2 + size.bit_length() - 1
+    count = len(shapes)
+    scratch = [bf(t_len, d_model), bf(s_len, d_model), bf(d_model, 2 * d_model), bf(d_model, 2 * d_model)]
+    scratch += [bf(own, d_model)] * 8 + [bf(own, ff)] * 2 + [bf(own, d_model)] * 2 + [
+        fl(own, d_model), bf(4, t_len, 256), bf(4, s_len, 256),
+        fl(t_len, d_model), bf(t_len, d_model), bf(2, t_len // 4, d_model),
+        fl(s_len, d_model), bf(s_len, d_model), bf(2, s_len // 4, d_model),
+        bf(2, t_len // 4, d_model), fl(levels + 1, 24, d_model), fl(levels, 24, d_model),
+    ]
+    scratch += [fl(2, rows, q) for rows, _, q in shapes]
+    scratch += [bf(2, rows, q) for rows, _, q in shapes] * 2
+    scratch += [bf(2, size - 1, block, q) for _, block, q in shapes] * 2
+    scratch += [bf(2, block, q) for _, block, q in shapes]
+    scratch += [dma((24,)), dma((16,)), dma((count, 2, size)), dma((count, 2, size)), dma((count,)), dma((count,)),
+                dma((count, 3)), dma((count, 3)), dma((7,)), dma((7,)), dma((levels,)), dma((levels,)), dma((6,)),
+                dma((3,))]
+    return pl.pallas_call(
+        functools.partial(settle_kernel, size, shapes),
+        out_shape=out_shape,
+        in_specs=[any_spec] * 19,
+        out_specs=[any_spec] * len(out_shape),
+        scratch_shapes=scratch,
+        compiler_params=pltpu.CompilerParams(
+            collective_id=1, has_side_effects=True, vmem_limit_bytes=64 * 1024 * 1024 - 512 * 1024),
+        name="settle",
+    )(x_full, m_full, w_all, layer_rows, mixed, self_low, first_low, cdq, cmixed, cross_low, second_low, up_low,
+      active, down_low, dq, part, dkv, dckv, vec_sums)
+
+
+def finish_kernel(factor, lo, dt, dm, *refs):
+    ga, gb = refs[:5], refs[5:10]
+    lo_out, dt_out, dm_out, qkv, out, cq, pair, cout, up, down = refs[10:]
+    lo_out[...] = lo[...]
+    dt_out[...] = dt[...]
+    dm_out[...] = dm[...]
+    targets = ([down], [up], [(qkv, 0), (qkv, 1), (qkv, 2)], [(pair, 0), (pair, 1)], [out, cq, cout])
+    for s, pieces in enumerate(targets):
+        for half in range(2):
+            for way in range(2):
+                total = (ga[s][half, way].astype(F32) + gb[s][half, way].astype(F32)) * factor
+                width = total.shape[1] // len(pieces)
+                for p, target in enumerate(pieces):
+                    ref, slot = target if isinstance(target, tuple) else (target, 0)
+                    column = slot * 4 * width + (2 * half + way) * width
+                    ref[:, column:column + width] = total[:, p * width:(p + 1) * width]
+
+
+def finish_fused(settled, factor, d_model, ff):
+    lo, dt, dm, vec_sums = settled[:4]
+    size = lax.axis_size("dp")
+    block = d_model // size
+    rows = [jax.ShapeDtypeStruct(a.shape, BF16) for a in (lo, dt, dm)]
+    grads = [jax.ShapeDtypeStruct((block, n * d_model), F32) for n in (3, 1, 1, 2, 1)]
+    grads += [jax.ShapeDtypeStruct((block, ff), F32), jax.ShapeDtypeStruct((ff // size, d_model), F32)]
+    vmem = pl.BlockSpec(memory_space=pltpu.VMEM)
+    done = pl.pallas_call(
+        functools.partial(finish_kernel, factor),
+        out_shape=rows + grads,
+        in_specs=[vmem] * 13,
+        out_specs=[vmem] * 10,
+        compiler_params=pltpu.CompilerParams(vmem_limit_bytes=32 * 1024 * 1024),
+        name="finish",
+    )(lo, dt, dm, *settled[4:])
+    vec_sums = jnp.concatenate([vec_sums, jnp.zeros((8, d_model), F32)], axis=0) * factor
+    return (done[0][:, None], done[1][:, None], done[2][:, None], *done[3:], *unpack_vectors(vec_sums, d_model))
 
 
 def pack_vectors(proj_bias, up_bias, norm_gain, norm_bias, d_model):
@@ -404,9 +984,10 @@
         return lax.all_gather(lax.squeeze(rows, (1,)), "seq", axis=1, tiled=True)[micro]
 
     weights = [lax.all_gather(shard, "dp", axis=0, tiled=True) for shard in shards]
-    vec = lax.psum(packed, "dp").astype(F32)
-    bounds = lax.psum(counts, "seq")[micro]
-    return whole(tokens), whole(memory), whole(cotangent), bounds, vec, weights
+    vec_all = lax.psum(packed, "dp")[None]
+    bounds = lax.psum(counts[:, 0, 0], "seq")[micro]
+    w_all = jnp.concatenate(weights[:6], axis=1)
+    return whole(tokens), whole(memory), whole(cotangent), bounds, vec_all, w_all, weights[6]
 
 
 def own_rows(rows, core):
@@ -421,7 +1002,7 @@
     return blocks.reshape(rows.shape[0] * 2, rows.shape[1])
 
 
-def settle_plain(x_full, m_full, weights, results, factor):
+def settle_plain(x_full, m_full, w_all, results, factor):
     (layer_rows, mixed, self_low, first_low, cdq, cmixed, cross_low, second_low, up_low, active, down_low, dq,
      part, dkv, dckv, vec_sums) = results
     place = lax.axis_index("seq")
@@ -429,8 +1010,8 @@
     d_model = x_full.shape[1]
     dkv = jnp.moveaxis(dkv, 0, 1).reshape(x_full.shape[0], 2 * d_model)
     dckv = jnp.moveaxis(dckv, 0, 1).reshape(m_full.shape[0], 2 * d_model)
-    input_rows = spread_rows(part, core) + mm_nt(dkv, weights[0][:, d_model:])
-    memory_rows = mm_nt(dckv, weights[3])
+    input_rows = spread_rows(part, core) + mm_nt(dkv, w_all[:, d_model:3 * d_model])
+    memory_rows = mm_nt(dckv, w_all[:, 5 * d_model:7 * d_model])
 
     def home(rows):
         both = jnp.stack([rows, jnp.zeros_like(rows)])
@@ -462,13 +1043,23 @@
     tgt_counts = jnp.sum(tgt_segments[:, 0, :, None] < docs, axis=1, dtype=jnp.int32)
     src_counts = jnp.sum(src_segments[:, 0, :, None] < docs[1:], axis=1, dtype=jnp.int32)
     counts = jnp.concatenate([tgt_counts, src_counts], axis=1)
+    counts = jnp.pad(counts[:, None, None], ((0, 0), (0, 0), (0, 7), (0, 128 - counts.shape[1])))
     packed = pack_vectors(proj_bias, up_bias, norm_gain, norm_bias, d_model)
-    x_full, m_full, ct_full, bounds, vec, weights = gather_plain(
-        tokens, memory, cotangent, counts, packed, shards)
-    bounds = jnp.concatenate([core.astype(jnp.int32)[None], bounds, jnp.zeros((2,), jnp.int32)])
-    results = run_layer(bounds, x_full, m_full, ct_full, vec, weights)
-    row_total = MB * lax.axis_size("dp") * tokens.shape[2] * lax.axis_size("seq")
-    return settle_plain(x_full, m_full, weights, results, 1.0 / math.sqrt(row_total))
+    size, rows = lax.axis_size("dp"), self_qkv.shape[0]
+    fused = rows % 64 == 0 and size & (size - 1) == 0 and size > 2
+    factor = 1.0 / math.sqrt(MB * size * tokens.shape[2] * lax.axis_size("seq"))
+    if fused:
+        x_full, m_full, ct_full, counts, vec_all, w_all, w_down = gather_fused(
+            tokens, memory, cotangent, counts, packed, shards)
+        bounds = jnp.sum(counts.reshape(-1, 8, 128), axis=0)[0]
+    else:
+        x_full, m_full, ct_full, bounds, vec_all, w_all, w_down = gather_plain(
+            tokens, memory, cotangent, counts, packed, shards)
+    bounds = jnp.concatenate([core.astype(jnp.int32)[None], bounds[:19]])
+    results = run_layer(bounds, x_full, m_full, ct_full, vec_all, w_all, w_down)
+    if fused:
+        return finish_fused(settle_fused(x_full, m_full, w_all, results), factor, d_model, ffn_up.shape[1])
+    return settle_plain(x_full, m_full, w_all, results, factor)
 
 
 def solution(mesh):

time: 1290 us -> 244 us (0.19)
  waiting for transfers between devices: 944 us -> 0 us
  blocking collectives: 145 us -> 0 us
  Pallas kernels: 88.2 us -> 219 us
  other arithmetic: 33.2 us -> 2.62 us
  matrix products: 24.6 us -> 0 us
  local copies, waits for them, and re-layouts: 32.8 us -> 18.4 us
  between operations: 14.9 us -> 0.79 us
    reduce_scatter x10 -> x0, waiting for transfers between devices: 662 us -> none  [the longest x7 507 us: settle_plain(): lax.psum_scatter(grad, 'dp', scatter_dimension=0, tiled=True)]
    psum x2 -> x0, waiting for transfers between devices: 162 us -> none  [the longest x1 109 us: settle_plain(): vec_sums = lax.psum(vec_sums, ('dp', 'seq')) * factor]
    pallas_call x0 -> x3, Pallas kernels: none -> 138 us  [the longest x1 82.8 us: settle_fused(): pl.pallas_call(functools.partial(settle_kernel, size, shapes), out_shape=...]
    all_gather x7 -> x0, waiting for transfers between devices: 114 us -> none  [the longest x4 114 us: gather_plain(): lax.all_gather(shard, 'dp', axis=0, tiled=True)]
    all_gather x3 -> x0, blocking collectives: 101 us -> none  [gather_plain(): lax.all_gather(shard, 'dp', axis=0, tiled=True)]
    psum x2 -> x0, blocking collectives: 44 us -> none  [the longest x1 39.1 us: gather_plain(): vec = lax.psum(packed, 'dp').astype(F32)]
    dot_general x10 -> x0, matrix products: 24.6 us -> none  [the longest x8 21.4 us: mm_tn(): lax.dot_general(left, right, (((0,), (0,)), ((), ())), preferred_element_...]
  transfers between devices with their start and end apart: 19 -> 0, of which waited for: 15 -> 0; matrix products, arithmetic and copies ran while one was open for 6% -> 0% of each run, Pallas kernels for 0% -> 0%
where the time goes in v2:
time: 244 us; the launch traced here: 241 us
  Pallas kernels  219 us (90%)
  local copies, waits for them, and re-layouts  18.4 us (8%)
  other arithmetic  2.62 us (1%)
    pallas_call x1, Pallas kernels, settle_fused(): pl.pallas_call(functools.partial(settle_kernel, size, shapes), out_shape=...  82.8 us
    pallas_call x1, Pallas kernels, run_layer(): pl.pallas_call(layer_kernel, out_shape=out_shape, grid_spec=pltpu.Prefetc...  81.1 us
    pallas_call x1, Pallas kernels, gather_fused(): pl.pallas_call(functools.partial(gather_kernel, size, splits), out_shape=...  53.2 us
    unnamed x34, local copies, waits for them, and re-layouts  14 us

profile of v2, /device:TPU:0, one launch (start us, length us, event | category | flops | bytes accessed | tf_op | source)
XLA Modules:
  0.0 241.2 jit_solution(5358818558353191844)
XLA Ops:
  0.7 0.8 pad_maximum_fusion
  1.5 0.5 dynamic_update_slice.9
  2.1 0.9 dynamic_update_slice.10
  3.0 0.1 dynamic_update_slice.11.packed
  3.1 0.7 copy.50
  3.8 0.2 fusion
  4.1 0.1 copy.40
  4.2 0.7 copy.51
  4.9 0.2 convert_reduce_fusion
  5.2 0.6 pad.5.counts
  5.8 53.2 %gather.1 = (bf16[1536,512]{1,0:T(8,128)(2,1)}, bf16[1024,512]{1,0:T(8,128)(2,1)}, bf16[1536,512]{1,0:T(8,128)(2,1)}, s32[32,128]{1,0:T(8,128)}, bf16[8,32,512]{...) custom-call(bf16[2,1,384,512]{3,2,1,0:T(8,128)(2,1)} %tokens.1, ...), custom_call_target="tpu_custom_call" | custom-call | tf_op jit(solution)/shard_map/gather/pallas_call | solution.py:529
  59.0 0.7 bitcast_reduce_fusion
  59.8 0.6 pad_add_fusion.1.bounds
  60.4 81.1 %layer.1 = (bf16[768,512]{1,0:T(8,128)(2,1)}, bf16[768,512]{1,0:T(8,128)(2,1)}, bf16[768,512]{1,0:T(8,128)(2,1)}, bf16[768,512]{1,0:T(8,128)(2,1)}, bf16[768,512...) custom-call(s32[20]{0:T(128)} %pad_add_fusion.1.bounds, ...), custom_call_target="tpu_custom_call" | custom-call | tf_op jit(solution)/shard_map/layer/pallas_call | solution.py:370
  141.4 82.8 %settle.1 = (bf16[2,384,512]{2,1,0:T(8,128)(2,1)}, bf16[2,384,512]{2,1,0:T(8,128)(2,1)}, bf16[2,256,512]{2,1,0:T(8,128)(2,1)}, f32[24,512]{1,0:T(8,128)}, bf16[2...) custom-call(bf16[1536,512]{1,0:T(8,128)(2,1)} %get-tuple-element.61., ...), custom_call_target="tpu_custom_call" | custom-call | tf_op jit(solution)/shard_map/settle/pallas_call | solution.py:912
  224.3 1.1 copy-done
  225.4 1.1 copy-done.1
  226.5 1.0 copy-done.2
  227.6 0.9 copy-done.3
  228.5 0.9 copy-done.4
  229.5 0.9 copy-done.5
  230.4 0.9 copy-done.6
  231.4 0.9 copy-done.7
  232.3 0.9 copy-done.8
  233.2 0.9 copy-done.9
  234.1 0.9 copy-done.10
  235.1 0.9 copy-done.11
  236.0 0.9 copy-done.12
  236.9 2.3 finish.1
  239.2 0.6 dynamic_slice.7
  239.9 0.7 fusion.1
  240.5 0.7 constant_dynamic-slice_fusion
  (29 shorter events, 0.3 us)
Async XLA Ops:
  3.1 2.7 %copy-start.13 = (bf16[32,512]{1,0:T(8,128)(2,1)}, bf16[32,512]{1,0:T(8,128)(2,1)S(1)}, u32[]{:S(2)}) copy-start(bf16[32,512]{1,0:T(8,128)(2,1)S(1)} %dynamic_update_slice.11.packed) | copy-start | bytes 98308
  224.2 1.1 copy-start
  225.4 1.1 copy-start.1
  226.5 1.0 copy-start.2
  227.6 0.9 copy-start.3
  228.5 0.9 copy-start.4
  229.5 0.9 copy-start.5
  230.4 0.9 copy-start.6
  231.4 0.9 copy-start.7
  232.3 0.9 copy-start.8
  233.2 0.9 copy-start.9
  234.1 0.9 copy-start.10
  235.1 0.9 copy-start.11
  236.0 0.9 copy-start.12
  236.9 2.3 copy-start.14

commit v3 on v2

--- a/solution.py
+++ b/solution.py
@@ -56,7 +56,7 @@
 
 
 def layer_kernel(
-    bounds,
+    counts,
     x_hbm, m_hbm, x_ref, ct_ref, vec_all, w_hbm, wdown_hbm,
     layer_out, mixed_out, self_low_out, first_low_out, cdq_out, cmixed_out, cross_low_out,
     second_low_out, up_low_out, active_out, down_low_out, dq_out, part_out,
@@ -64,7 +64,7 @@
     wqkv, wout, wcq, wckv, wcout, wup, wdown,
     k_s, kt_s, v_s, vt_s, k_c, kt_c, v_c, vt_c,
     p_s, p_c, dk_s, dv_s, dk_c, dv_c,
-    qm_s, qm_c, gtm, gm, ot_s, ot_c, dqt, slope_s, vec_ref, sems,
+    qm_s, qm_c, gtm, gm, ot_s, ot_c, dqt, slope_s, vec_ref, kn_s, kn_c, sems,
 ):
     step = pl.program_id(0)
     steps = pl.num_programs(0)
@@ -72,7 +72,9 @@
     s_len = k_c.shape[0]
     ff = wup.shape[1]
     hd = d_model // H
-    core = bounds[0]
+    core = counts[32, 0]
+    tgt_starts = [0] + [counts[0, d] + counts[8, d] + counts[16, d] + counts[24, d] for d in range(1, 9)]
+    src_starts = [0] + [counts[0, d] + counts[8, d] + counts[16, d] + counts[24, d] for d in range(9, 17)]
     block = 2 * step + core
 
     def columns(start, count):
@@ -90,7 +92,7 @@
 
     @pl.when(step == 0)
     def _():
-        for load in loads:
+        for load in loads[:6]:
             load.start()
         dk_s[...] = jnp.zeros_like(dk_s)
         dv_s[...] = jnp.zeros_like(dv_s)
@@ -101,7 +103,8 @@
         vec = vec_ref[...]
         vec_t = vec.T
 
-        def project(rows_ref, w_ref, k_at, kt, k, vt, v, bias_row, bias_row_t, count):
+        def project(rows_ref, w_ref, k_at, kt, k, vt, v, norms, bias_row, bias_row_t, count):
+            norms[...] = jnp.zeros_like(norms)
             wk = w_ref[:, k_at:k_at + d_model]
             wv = w_ref[:, k_at + d_model:k_at + 2 * d_model]
             wk_t = wk.T
@@ -112,7 +115,12 @@
                 rows = jnp.concatenate([rows_ref[0, at, :], rows_ref[1, at, :]], axis=1)
                 k[at, :] = mm(rows, wk).astype(BF16)
                 v[at, :] = (mm(rows, wv) + bias_row).astype(BF16)
-                kt[:, at] = mm_nt(wk_t, rows).astype(BF16)
+                keys_t = mm_nt(wk_t, rows)
+                kt[:, at] = keys_t.astype(BF16)
+                squares = keys_t * keys_t
+                for h in range(H):
+                    own = jnp.sum(fold(squares[h * hd:(h + 1) * hd], jnp.sum), axis=0, keepdims=True)
+                    norms[h:h + 1, :] = jnp.maximum(norms[h:h + 1, :], own)
                 vt[:, at] = (mm_nt(wv_t, rows) + bias_row_t).astype(BF16)
                 return carry
 
@@ -120,10 +128,12 @@
 
         for load in loads[:3]:
             load.wait()
-        project(p_s, wqkv, d_model, kt_s, k_s, vt_s, v_s, vec[1:2], vec_t[:, 1:2], t_len)
+        for load in loads[6:]:
+            load.start()
+        project(p_s, wqkv, d_model, kt_s, k_s, vt_s, v_s, kn_s, vec[1:2], vec_t[:, 1:2], t_len)
         for load in loads[3:6]:
             load.wait()
-        project(p_c, wckv, 0, kt_c, k_c, vt_c, v_c, vec[4:5], vec_t[:, 4:5], s_len)
+        project(p_c, wckv, 0, kt_c, k_c, vt_c, v_c, kn_c, vec[4:5], vec_t[:, 4:5], s_len)
         for load in loads[6:]:
             load.wait()
 
@@ -131,28 +141,30 @@
 
     qpos = block * RB + lax.broadcasted_iota(jnp.int32, (1, RB), 1)
     lo_s = jnp.zeros((1, RB), jnp.int32)
-    hi_s = jnp.full((1, RB), bounds[2], jnp.int32)
+    hi_s = jnp.full((1, RB), tgt_starts[1], jnp.int32)
     lo_c = jnp.zeros((1, RB), jnp.int32)
-    hi_c = jnp.full((1, RB), bounds[2 + 8], jnp.int32)
+    hi_c = jnp.full((1, RB), src_starts[1], jnp.int32)
     for doc in range(1, 8):
-        inside = qpos >= bounds[1 + doc]
-        lo_s = jnp.where(inside, bounds[1 + doc], lo_s)
-        hi_s = jnp.where(inside, bounds[2 + doc], hi_s)
-        lo_c = jnp.where(inside, bounds[9 + doc], lo_c)
-        hi_c = jnp.where(inside, bounds[10 + doc], hi_c)
+        inside = qpos >= tgt_starts[doc]
+        lo_s = jnp.where(inside, tgt_starts[doc], lo_s)
+        hi_s = jnp.where(inside, tgt_starts[doc + 1], hi_s)
+        lo_c = jnp.where(inside, src_starts[doc], lo_c)
+        hi_c = jnp.where(inside, src_starts[doc + 1], hi_c)
     first = block * RB
     last = first + RB - 1
-    s_from, s_to, c_from, c_to = 0, bounds[2], 0, bounds[10]
+    s_from, s_to, c_from, c_to = 0, tgt_starts[1], 0, src_starts[1]
     for doc in range(1, 8):
-        in_first = first >= bounds[1 + doc]
-        in_last = last >= bounds[1 + doc]
-        s_from = jnp.where(in_first, bounds[1 + doc], s_from)
-        c_from = jnp.where(in_first, bounds[9 + doc], c_from)
-        s_to = jnp.where(in_last, bounds[2 + doc], s_to)
-        c_to = jnp.where(in_last, bounds[10 + doc], c_to)
-
-    def block_range(start, stop):
-        return lax.div(start, KB), lax.div(stop + (KB - 1), KB)
+        in_first = first >= tgt_starts[doc]
+        in_last = last >= tgt_starts[doc]
+        s_from = jnp.where(in_first, tgt_starts[doc], s_from)
+        c_from = jnp.where(in_first, src_starts[doc], c_from)
+        s_to = jnp.where(in_last, tgt_starts[doc + 1], s_to)
+        c_to = jnp.where(in_last, src_starts[doc + 1], c_to)
+
+    def block_range(start, stop, length):
+        base = lax.div(start, 128) * 128
+        count = lax.div(stop - base + (KB - 1), KB)
+        return jnp.minimum(base, length - count * KB), count
 
     def halves(values, axis, h):
         place = lax.broadcasted_iota(jnp.int32, values.shape, axis)
@@ -164,11 +176,23 @@
             natural[h] = halves(rows[:, pair], 1, h)
             transposed[h] = halves(rows_t[pair, :], 0, h)
 
-    def attend(qtm, k, vt, p, ot, lo, hi, start, stop):
-        j_from, j_to = block_range(start, stop)
+    def key_rows(base, j):
+        return pl.ds(pl.multiple_of(base + j * KB, 128), KB)
+
+    def attend(query_t, qtm, k, vt, p, ot, norms, lo, hi, start, stop):
+        base, count = block_range(start, stop, k.shape[0])
+        squares = query_t.astype(F32)
+        squares = squares * squares
+        bound = None
+        for h in range(H):
+            own = jnp.sum(fold(squares[h * hd:(h + 1) * hd], jnp.sum), axis=0, keepdims=True)
+            own = own * jnp.max(norms[h:h + 1, :], axis=1, keepdims=True)
+            bound = own if bound is None else jnp.maximum(bound, own)
+        small = jnp.max(bound) <= 3600.0
+        shifts = jnp.where(small, 0, count)
 
         def bias_of(j):
-            kpos = j * KB + lax.broadcasted_iota(jnp.int32, (KB, RB), 0)
+            kpos = base + j * KB + lax.broadcasted_iota(jnp.int32, (KB, RB), 0)
             return jnp.where((kpos >= lo) & (kpos < hi), 0.0, -1e30).astype(F32)
 
         def scores(h, at, bias):
@@ -176,16 +200,17 @@
             return mm(k[at, pair], qtm[h]) + bias
 
         def top(j, highest):
-            at = pl.ds(pl.multiple_of(j * KB, KB), KB)
+            at = key_rows(base, j)
             bias = bias_of(j)
             return tuple(jnp.maximum(highest[h], fold(scores(h, at, bias), jnp.max)) for h in range(H))
 
-        highest = lax.fori_loop(j_from, j_to, top, tuple(jnp.full((8, RB), -1e30, F32) for _ in range(H)))
+        lowest = jnp.full((8, RB), jnp.where(small, 0.0, -1e30), F32)
+        highest = lax.fori_loop(0, shifts, top, (lowest,) * H)
         highest = [jnp.max(part, axis=0, keepdims=True) for part in highest]
         ot[...] = jnp.zeros_like(ot)
 
         def gather(j, totals):
-            at = pl.ds(pl.multiple_of(j * KB, KB), KB)
+            at = key_rows(base, j)
             bias = bias_of(j)
             out = []
             sc = [scores(h, at, bias) for h in range(H)]
@@ -201,7 +226,7 @@
                 ot[head, :] += mm(vt[head, at], lows[h])
             return tuple(out)
 
-        totals = lax.fori_loop(j_from, j_to, gather, tuple(jnp.zeros((8, RB), F32) for _ in range(H)))
+        totals = lax.fori_loop(0, count, gather, (jnp.zeros((8, RB), F32),) * H)
         inverse = []
         for h in range(H):
             inv = 1.0 / jnp.sum(totals[h], axis=0, keepdims=True)
@@ -211,7 +236,7 @@
         return inverse
 
     def attend_back(grad_rows, inverse, qm, k, kt, v, p, ot, dk, dv, start, stop):
-        j_from, j_to = block_range(start, stop)
+        base, count = block_range(start, stop, k.shape[0])
         grad_t = grad_rows.T.astype(F32)
         scaled_t = []
         spread = []
@@ -225,7 +250,7 @@
         dqt[...] = jnp.zeros_like(dqt)
 
         def body(j, carry):
-            at = pl.ds(pl.multiple_of(j * KB, KB), KB)
+            at = key_rows(base, j)
             pairs = [slice((h // 2) * 2 * hd, (h // 2 + 1) * 2 * hd) for h in range(H)]
             prob_grads = [mm(v[at, pairs[h]], gtm[h]) for h in range(H)]
             for h in range(0, H, 2):
@@ -238,7 +263,7 @@
                 dqt[head, :] += mm(kt[head, at], lows[h])
             return carry
 
-        lax.fori_loop(j_from, j_to, body, 0)
+        lax.fori_loop(0, count, body, 0)
         return dqt[...].astype(BF16).T
 
     def add_vec(row, values):
@@ -246,8 +271,9 @@
 
     x_rows = x_ref[...]
     q = ((mm(x_rows, wqkv[:, :d_model]) + vec[0:1]) * 0.125).astype(BF16)
-    put_masked(q, q.T, qm_s, gtm)
-    inv_s = attend(gtm, k_s, vt_s, p_s, ot_s, lo_s, hi_s, s_from, s_to)
+    q_t = q.T
+    put_masked(q, q_t, qm_s, gtm)
+    inv_s = attend(q_t, gtm, k_s, vt_s, p_s, ot_s, kn_s, lo_s, hi_s, s_from, s_to)
     mixed = ot_s[...].astype(BF16).T
     mixed_out[...] = mixed
     first_norm, unit1, scale1 = normalize(
@@ -255,8 +281,9 @@
     first_low = first_norm.astype(BF16)
     first_low_out[...] = first_low
     cq = ((mm(first_low, wcq[...]) + vec[3:4]) * 0.125).astype(BF16)
-    put_masked(cq, cq.T, qm_c, gtm)
-    inv_c = attend(gtm, k_c, vt_c, p_c, ot_c, lo_c, hi_c, c_from, c_to)
+    cq_t = cq.T
+    put_masked(cq, cq_t, qm_c, gtm)
+    inv_c = attend(cq_t, gtm, k_c, vt_c, p_c, ot_c, kn_c, lo_c, hi_c, c_from, c_to)
     cmixed = ot_c[...].astype(BF16).T
     cmixed_out[...] = cmixed
     second, unit2, scale2 = normalize(
@@ -300,6 +327,19 @@
     cross_grad = mm_nt(cross_low, wcout[...]).astype(BF16)
     cdq = attend_back(cross_grad, inv_c, qm_c, k_c, kt_c, v_c, p_c, ot_c, dk_c, dv_c, c_from, c_to) * 0.125
     cdq_out[...] = cdq
+
+    def put_out(slabs, dk, dv):
+        for n in range(2):
+            cols = slice(n * 256, (n + 1) * 256)
+            slabs[n] = dk[:, cols].astype(BF16)
+            slabs[2 + n] = dv[:, cols].astype(BF16)
+
+    @pl.when(step == steps - 1)
+    def _():
+        add_vec(4, dv_c[...])
+        put_out(p_c, dk_c, dv_c)
+        pltpu.make_async_copy(p_c.at[0:4], dckv_hbm, sems.at[1]).start()
+
     add_vec(3, cdq.astype(F32))
     grad_first = grad_mid + mm_nt(cdq, wcq[...])
     add_vec(11, grad_first * unit1)
@@ -317,24 +357,13 @@
     @pl.when(step == steps - 1)
     def _():
         add_vec(1, dv_s[...])
-        add_vec(4, dv_c[...])
-        for n in range(2):
-            cols = slice(n * 256, (n + 1) * 256)
-            p_s[n] = dk_s[:, cols].astype(BF16)
-            p_s[2 + n] = dv_s[:, cols].astype(BF16)
-            p_c[n] = dk_c[:, cols].astype(BF16)
-            p_c[2 + n] = dv_c[:, cols].astype(BF16)
-        stores = [
-            pltpu.make_async_copy(p_s.at[0:4], dkv_hbm, sems.at[0]),
-            pltpu.make_async_copy(p_c.at[0:4], dckv_hbm, sems.at[1]),
-        ]
-        for store in stores:
-            store.start()
-        for store in stores:
-            store.wait()
-
-
-def run_layer(bounds, x_full, m_full, ct_full, vec_all, w_all, w_down):
+        put_out(p_s, dk_s, dv_s)
+        pltpu.make_async_copy(p_s.at[0:4], dkv_hbm, sems.at[0]).start()
+        pltpu.make_async_copy(p_s.at[0:4], dkv_hbm, sems.at[0]).wait()
+        pltpu.make_async_copy(p_c.at[0:4], dckv_hbm, sems.at[1]).wait()
+
+
+def run_layer(counts, x_full, m_full, ct_full, vec_all, w_all, w_down):
     t_len, d_model = x_full.shape
     s_len = m_full.shape[0]
     ff = w_down.shape[0]
@@ -364,7 +393,7 @@
         bf(H, t_len, RB), bf(H, s_len, RB),
         fl(t_len, d_model), fl(t_len, d_model), fl(s_len, d_model), fl(s_len, d_model),
         bf(H, RB, 128), bf(H, RB, 128), bf(H, 128, RB), bf(H, RB, 128),
-        fl(d_model, RB), fl(d_model, RB), fl(d_model, RB), fl(RB, ff), fl(32, d_model),
+        fl(d_model, RB), fl(d_model, RB), fl(d_model, RB), fl(RB, ff), fl(32, d_model), fl(H, RB), fl(H, RB),
         pltpu.SemaphoreType.DMA((11,)),
     ]
     return pl.pallas_call(
@@ -373,14 +402,14 @@
         grid_spec=pltpu.PrefetchScalarGridSpec(
             num_scalar_prefetch=1,
             grid=(steps,),
-            in_specs=[any_spec, any_spec] + [pl.BlockSpec((RB, d_model), lambda i, b: (2 * i + b[0], 0))] * 2 + [
+            in_specs=[any_spec, any_spec] + [pl.BlockSpec((RB, d_model), lambda i, b: (2 * i + b[32, 0], 0))] * 2 + [
                       pl.BlockSpec(vec_all.shape, lambda i, b: (0, 0, 0)), any_spec, any_spec],
             out_specs=out_specs,
             scratch_shapes=scratch,
         ),
         compiler_params=pltpu.CompilerParams(vmem_limit_bytes=64 * 1024 * 1024 - 512 * 1024),
         name="layer",
-    )(bounds, x_full, m_full, x_full, ct_full, vec_all, w_all, w_down)
+    )(counts, x_full, m_full, x_full, ct_full, vec_all, w_all, w_down)
 
 
 def ring_neighbours(at, size):
@@ -401,9 +430,10 @@
 
 def gather_kernel(
     size, splits,
-    tokens, memory, cotangent, counts, packed, w_qkv, w_out, w_cq, w_ckv, w_cout, w_up, w_down,
+    tokens, memory, cotangent, tgt_ids, src_ids, proj_bias, up_bias, norm_gain, norm_bias,
+    w_qkv, w_out, w_cq, w_ckv, w_cout, w_up, w_down,
     x_full, m_full, c_full, counts_all, vec_all, w_all, d_all,
-    send_ring, recv_ring, send_core, recv_core, local_sems, send_rows, recv_rows,
+    counts, spread, packed, send_ring, recv_ring, send_core, recv_core, local_sems, send_rows, recv_rows,
 ):
     at, place = lax.axis_index("dp"), lax.axis_index("seq")
     micro, core = lax.div(place, 2), lax.rem(place, 2)
@@ -417,6 +447,32 @@
     for peer in peers:
         pl.semaphore_signal(barrier, inc=1, device_id=peer, device_id_type=pl.DeviceIdType.MESH)
 
+    d_model = spread.shape[1]
+    width = proj_bias.shape[1]
+
+    def put(row, values, start, length):
+        cols = lax.broadcasted_iota(jnp.int32, (length, d_model), 1)
+        ones = lax.broadcasted_iota(jnp.int32, (length, d_model), 0) + start == cols
+        spread[row:row + values.shape[0], :] = mm(values, jnp.where(ones, 1.0, 0.0).astype(BF16))
+
+    spread[...] = jnp.zeros_like(spread)
+    put(0, proj_bias[...], at * width, width)
+    for n in range(4):
+        put(7 + n, up_bias[...], at * 4 * width - n * d_model, 4 * width)
+    put(11, norm_gain[...], at * width, width)
+    put(14, norm_bias[...], at * width, width)
+    packed[...] = spread[...].astype(BF16)
+    lane = lax.broadcasted_iota(jnp.int32, (8, 128), 1)
+    for index in range(2):
+        total = jnp.zeros((8, 128), F32)
+        for ids, docs, offset in ((tgt_ids, range(1, 9), 0), (src_ids, range(1, 9), 8)):
+            row = ids[index]
+            for doc in docs:
+                below = jnp.sum(jnp.where(row < doc, 1.0, 0.0), axis=1, keepdims=True)
+                total = total + jnp.where(lane == doc + offset, below, 0.0)
+        counts[index, 0] = total.astype(jnp.int32)
+    counts[2, 0] = jnp.full((8, 128), core, jnp.int32)
+
     wide, tall = w_qkv.shape[0], w_down.shape[0]
     local = []
     for n, (shard, column) in enumerate(zip((w_qkv, w_out, w_cq, w_ckv, w_cout, w_up), splits)):
@@ -424,6 +480,7 @@
             shard, w_all.at[pl.ds(at * wide, wide), pl.ds(column, shard.shape[1])], local_sems.at[n]))
     local.append(pltpu.make_async_copy(w_down, d_all.at[pl.ds(at * tall, tall)], local_sems.at[6]))
     local.append(pltpu.make_async_copy(packed, vec_all.at[at], local_sems.at[7]))
+    local.append(pltpu.make_async_copy(counts.at[2, 0], counts_all.at[pl.ds(32, 8)], local_sems.at[12]))
     for copy in local:
         copy.start()
 
@@ -511,7 +568,7 @@
         copy.wait_send()
 
 
-def gather_fused(tokens, memory, cotangent, counts, packed, shards):
+def gather_fused(tokens, memory, cotangent, tgt_ids, src_ids, vectors, shards):
     size = lax.axis_size("dp")
     d_model = tokens.shape[3]
     widths = [shard.shape[1] for shard in shards[:6]]
@@ -520,7 +577,7 @@
     any_spec = pl.BlockSpec(memory_space=pl.ANY)
     out_shape = [jax.ShapeDtypeStruct((seq * a.shape[2], d_model), BF16) for a in (tokens, memory, cotangent)]
     out_shape += [
-        jax.ShapeDtypeStruct((seq * 8, 128), jnp.int32),
+        jax.ShapeDtypeStruct((seq * 8 + 8, 128), jnp.int32),
         jax.ShapeDtypeStruct((size, 32, d_model), BF16),
         jax.ShapeDtypeStruct((size * shards[0].shape[0], sum(widths)), BF16),
         jax.ShapeDtypeStruct((size * shards[6].shape[0], d_model), BF16),
@@ -529,23 +586,24 @@
     return pl.pallas_call(
         functools.partial(gather_kernel, size, splits),
         out_shape=out_shape,
-        in_specs=[pl.BlockSpec(memory_space=pltpu.VMEM)] * 12,
+        in_specs=[pl.BlockSpec(memory_space=pltpu.VMEM)] * 16,
         out_specs=[any_spec] * 7,
-        scratch_shapes=[dma((3, 2, size)), dma((3, 2, size)), dma((2, 2, size)), dma((2, 2, size)), dma((12,)),
+        scratch_shapes=[pltpu.VMEM((3, 1, 8, 128), jnp.int32), pltpu.VMEM((32, d_model), F32), pltpu.VMEM((32, d_model), BF16),
+                        dma((3, 2, size)), dma((3, 2, size)), dma((2, 2, size)), dma((2, 2, size)), dma((13,)),
                         dma((4, 3)), dma((4, 3))],
         compiler_params=pltpu.CompilerParams(collective_id=0, has_side_effects=True),
         name="gather",
-    )(tokens, memory, cotangent, counts, packed, *shards)
+    )(tokens, memory, cotangent, tgt_ids, src_ids, *vectors, *shards)
 
 
 MESH = pl.DeviceIdType.MESH
-STREAMS = ("down", "up", "qkv", "pair", "outs")
+
+
+SCHEDULE = "D U r0 Q r1 P a0 O r2 a01 R r3 V a0123 H E a0123 V a0123 V a0123 V a0123 V a0123 a0123"
 
 
 def stream_shapes(d_model, ff, size):
-    quarters = (d_model // 4, ff // 4, 3 * d_model // 4, 2 * d_model // 4, 3 * d_model // 4)
-    rows = (ff, d_model, d_model, d_model, d_model)
-    return [(r, r // size, q) for r, q in zip(rows, quarters)]
+    return [(d_model, d_model // size, q) for q in (ff // 4, ff // 4, 5 * d_model // 4, 3 * d_model // 4)]
 
 
 def settle_kernel(size, shapes, *refs):
@@ -590,25 +648,35 @@
         copy.start()
         loads[name] = copy
 
-    load("vec", vec_hbm.at[pl.ds(0, 24)], vec_run.at[0])
-    load("active", active_hbm, active)
-    load("down_low", down_low_hbm, down_low)
-    load("second_low", second_low_hbm, second_low)
-    load("up_low", up_low_hbm, up_low)
-    load("dkv", dkv_hbm, dkv)
-    load("wkv", w_hbm.at[:, pl.ds(d_model, 2 * d_model)], wkv)
-    load("part", part_hbm, part)
-    load("dckv", dckv_hbm, dckv)
-    load("wpair", w_hbm.at[:, pl.ds(5 * d_model, 2 * d_model)], wpair)
-    load("xf", x_hbm, xf)
-    for n in range(t_len // (2 * RB)):
-        load(("xo", n), x_hbm.at[pl.ds((2 * n + core) * RB, RB)], xo.at[pl.ds(n * RB, RB)])
-    load("dq", dq_hbm, dq)
-    load("mf", m_hbm, mf)
-    for name, src, dst in (("mixed", mixed_hbm, mixed), ("self_low", self_low_hbm, self_low),
-                           ("first_low", first_low_hbm, first_low), ("cdq", cdq_hbm, cdq),
-                           ("cmixed", cmixed_hbm, cmixed), ("cross_low", cross_low_hbm, cross_low)):
-        load(name, src, dst)
+    def load_first():
+        load("active", active_hbm, active)
+        load("down_low", down_low_hbm, down_low)
+        load("vec", vec_hbm.at[pl.ds(0, 24)], vec_run.at[0])
+
+    def load_up():
+        load("second_low", second_low_hbm, second_low)
+        load("up_low", up_low_hbm, up_low)
+
+    def load_qkv():
+        load("dkv", dkv_hbm, dkv)
+        load("xf", x_hbm, xf)
+        for n in range(t_len // (2 * RB)):
+            load(("xo", n), x_hbm.at[pl.ds((2 * n + core) * RB, RB)], xo.at[pl.ds(n * RB, RB)])
+        load("dq", dq_hbm, dq)
+
+    def load_rest():
+        load("dckv", dckv_hbm, dckv)
+        load("mf", m_hbm, mf)
+        for name, src, dst in (("mixed", mixed_hbm, mixed), ("self_low", self_low_hbm, self_low),
+                               ("first_low", first_low_hbm, first_low), ("cdq", cdq_hbm, cdq),
+                               ("cmixed", cmixed_hbm, cmixed), ("cross_low", cross_low_hbm, cross_low)):
+            load(name, src, dst)
+        load("wkv", w_hbm.at[:, pl.ds(d_model, 2 * d_model)], wkv)
+        load("part", part_hbm, part)
+        load("wpair", w_hbm.at[:, pl.ds(5 * d_model, 2 * d_model)], wpair)
+
+    load_first()
+    load_up()
 
     pending = []
 
@@ -669,7 +737,7 @@
         store(rows_of(micro), home.at[micro])
         row_waits.append(send(rows_of(1 - micro), home.at[micro], row_ss.at[n], row_rs.at[n], chip_peer))
 
-    def split(values, pieces, s, rows):
+    def split(values, pieces, s, rows, base=0):
         width = values.shape[1] // pieces
         quarter = width // 4
         for p in range(pieces):
@@ -677,72 +745,83 @@
             upper = values[:, p * width + 2 * quarter:(p + 1) * width]
             own = jnp.where(core == 0, lower, upper)
             away = jnp.where(core == 0, upper, lower).astype(BF16)
+            cols = slice(base + p * quarter, base + (p + 1) * quarter)
             for way in range(2):
-                acc[s][way, rows, p * quarter:(p + 1) * quarter] = own[:, way * quarter:(way + 1) * quarter]
-                stage[s][way, rows, p * quarter:(p + 1) * quarter] = away[:, way * quarter:(way + 1) * quarter]
+                acc[s][way, rows, cols] = own[:, way * quarter:(way + 1) * quarter]
+                stage[s][way, rows, cols] = away[:, way * quarter:(way + 1) * quarter]
 
     core_waits = {}
-
-    def compute(s):
-        tile = 256
-        if s == 0:
-            loads["active"].wait()
-            loads["down_low"].wait()
-
-            def one(m, carry):
-                rows = pl.ds(pl.multiple_of(m * tile, tile), tile)
-                split(mm_tn(active[:, rows], down_low[...]), 1, s, rows)
-                return carry
-
-            lax.fori_loop(0, active.shape[1] // tile, one, 0)
-        elif s == 1:
-            loads["second_low"].wait()
-            loads["up_low"].wait()
-
-            def one(m, carry):
-                rows = pl.ds(pl.multiple_of(m * tile, tile), tile)
-                split(mm_tn(second_low[:, rows], up_low[...]), 1, s, rows)
-                return carry
-
-            lax.fori_loop(0, d_model // tile, one, 0)
-        elif s == 2:
-            loads["xf"].wait()
-            for n in range(t_len // (2 * RB)):
-                loads["xo", n].wait()
-            loads["dq"].wait()
-
-            def one(m, carry):
-                rows = pl.ds(pl.multiple_of(m * tile, tile), tile)
-                parts = [mm_tn(xo[:, rows], dq[...])]
-                whole = xf[:, rows]
-                parts += [mm_tn(whole, dkv[n]) for n in range(4)]
-                split(jnp.concatenate(parts, axis=1), 3, s, rows)
-                return carry
-
-            lax.fori_loop(0, d_model // tile, one, 0)
-        elif s == 3:
-            loads["mf"].wait()
-
-            def one(m, carry):
-                rows = pl.ds(pl.multiple_of(m * tile, tile), tile)
-                whole = mf[:, rows]
-                split(jnp.concatenate([mm_tn(whole, dckv[n]) for n in range(4)], axis=1), 2, s, rows)
-                return carry
-
-            lax.fori_loop(0, d_model // tile, one, 0)
-        else:
-            for name in ("mixed", "self_low", "first_low", "cdq", "cmixed", "cross_low"):
-                loads[name].wait()
-
-            def one(m, carry):
-                rows = pl.ds(pl.multiple_of(m * tile, tile), tile)
-                parts = [mm_tn(mixed[:, rows], self_low[...]), mm_tn(first_low[:, rows], cdq[...]),
-                         mm_tn(cmixed[:, rows], cross_low[...])]
-                split(jnp.concatenate(parts, axis=1), 3, s, rows)
-                return carry
-
-            lax.fori_loop(0, d_model // tile, one, 0)
+    tile = 256
+
+    def await_loads(*names):
+        for name in names:
+            loads[name].wait()
+
+    def each_tile(body):
+        def one(m, carry):
+            body(pl.ds(pl.multiple_of(m * tile, tile), tile))
+            return carry
+
+        lax.fori_loop(0, d_model // tile, one, 0)
+
+    def share(s):
         core_waits[s] = send(stage[s], other[s], core_ss.at[s], core_rs.at[s], core_peer)
+
+    def compute_down():
+        await_loads("active", "down_low")
+        load_qkv()
+        block, tall = shapes[0][1], active.shape[1] // size
+        quarter = d_model // 4
+
+        def one(m, carry):
+            values = mm_tn(active[:, pl.ds(pl.multiple_of(m * tall, tall), tall)], down_low[...])
+            rows = pl.ds(pl.multiple_of(m * block, block), block)
+            for n in range(tall // block):
+                split(values[n * block:(n + 1) * block], 1, 0, rows, n * quarter)
+            return carry
+
+        lax.fori_loop(0, size, one, 0)
+        share(0)
+
+    def compute_up():
+        await_loads("second_low", "up_low")
+        load_rest()
+        each_tile(lambda rows: split(mm_tn(second_low[:, rows], up_low[...]), 1, 1, rows))
+        share(1)
+
+    def compute_qkv():
+        await_loads("dkv", "xf", "dq", *(("xo", n) for n in range(t_len // (2 * RB))))
+
+        def one(rows):
+            split(mm_tn(xo[:, rows], dq[...]), 1, 2, rows)
+            whole = xf[:, rows]
+            for n in range(2):
+                parts = [mm_tn(whole, dkv[2 * n + m]) for m in range(2)]
+                split(jnp.concatenate(parts, axis=1), 1, 2, rows, (1 + n) * d_model // 4)
+
+        each_tile(one)
+
+    def compute_pair():
+        await_loads("dckv", "mf")
+
+        def one(rows):
+            whole = mf[:, rows]
+            for n in range(2):
+                parts = [mm_tn(whole, dckv[2 * n + m]) for m in range(2)]
+                split(jnp.concatenate(parts, axis=1), 1, 2, rows, (3 + n) * d_model // 4)
+
+        each_tile(one)
+        share(2)
+
+    def compute_outs():
+        await_loads("mixed", "self_low", "first_low", "cdq", "cmixed", "cross_low")
+
+        def one(rows):
+            for n, (left, right) in enumerate(((mixed, self_low), (first_low, cdq), (cmixed, cross_low))):
+                split(mm_tn(left[:, rows], right[...]), 1, 3, rows, n * d_model // 4)
+
+        each_tile(one)
+        share(3)
 
     ring_waits = {}
 
@@ -752,7 +831,7 @@
             core_waits[s].wait_recv()
         for way in range(2):
             owner = ring_member(mine - 1 - step if way == 0 else mine + 1 + step, size)
-            rows = pl.ds(owner * block, block)
+            rows = pl.ds(pl.multiple_of(owner * block, block), block)
             total = acc[s][way, rows, :] + other[s][way, rows, :].astype(F32)
             if step > 0:
                 ring_waits[s, way].wait_recv()
@@ -777,8 +856,7 @@
         tail.append(send(gb[s].at[core], gb[s].at[core], fin_ss.at[s, 2], fin_rs.at[s, 2], core_peer))
 
     def row_products():
-        for name in ("dkv", "wkv", "part", "dckv", "wpair"):
-            loads[name].wait()
+        await_loads("wkv", "part", "wpair")
 
         def tokens(b, carry):
             rows = pl.ds(pl.multiple_of(b * RB, RB), RB)
@@ -826,45 +904,45 @@
                 done[rows_at(k), :] = (full[rows_at(k), :] + got[k].astype(F32)).astype(BF16)
             home_rows(1 + n, lambda k, done=done, rows_at=rows_at: done.at[rows_at(k)], home)
 
-    compute(0)
-    ring(0, 0)
-    for copy in keep:
-        copy.wait()
-    for copy in give:
-        copy.wait_recv()
-    home_rows(0, lambda k: lo_buf.at[k], lo_home)
-    vec_step()
-    compute(1)
-    ring(1, 0)
-    ring(0, 1)
-    vec_step()
-    row_copies = row_products()
-    ring(0, 2)
-    row_finish(row_copies)
-    vec_step()
-    compute(2)
-    ring(2, 0)
-    ring(1, 1)
-    ring(0, 3)
-    vec_step()
-    compute(3)
-    ring(3, 0)
-    ring(2, 1)
-    ring(1, 2)
-    ring(0, 4)
-    vec_step()
-    compute(4)
-    ring(4, 0)
-    done = {0: 4, 1: 2, 2: 1, 3: 0, 4: 0}
-    while any(done[s] < size - 1 for s in range(count)):
-        for s in range(count - 1, -1, -1):
-            if done[s] < size - 1:
-                done[s] += 1
-                ring(s, done[s])
-                if done[s] == size - 1:
-                    finish(s)
-        while vec_state["level"] < len(vec_peers):
+    reached = [0] * count
+    sent_home = []
+
+    def advance(s):
+        if reached[s] < size - 1:
+            reached[s] += 1
+            ring(s, reached[s])
+            if reached[s] == size - 1:
+                finish(s)
+                sent_home.append(s)
+
+    def rows_start():
+        state["rows"] = row_products()
+
+    def rows_end():
+        row_finish(state["rows"])
+
+    def layer_rows():
+        for copy in keep:
+            copy.wait()
+        for copy in give:
+            copy.wait_recv()
+        home_rows(0, lambda k: lo_buf.at[k], lo_home)
+
+    def vectors():
+        if vec_state["level"] < len(vec_peers):
             vec_step()
+
+    state = {}
+    actions = {"D": compute_down, "U": compute_up, "Q": compute_qkv, "P": compute_pair, "O": compute_outs,
+               "R": rows_start, "E": rows_end, "H": layer_rows, "V": vectors}
+    for action in SCHEDULE.split():
+        if action in actions:
+            actions[action]()
+        elif action[0] == "r":
+            ring(int(action[1]), 0)
+        else:
+            for s in action[1:]:
+                advance(int(s))
     for s in range(count):
         forward(s)
     for copy in row_waits + tail:
@@ -922,42 +1000,63 @@
       active, down_low, dq, part, dkv, dckv, vec_sums)
 
 
-def finish_kernel(factor, lo, dt, dm, *refs):
-    ga, gb = refs[:5], refs[5:10]
-    lo_out, dt_out, dm_out, qkv, out, cq, pair, cout, up, down = refs[10:]
-    lo_out[...] = lo[...]
-    dt_out[...] = dt[...]
-    dm_out[...] = dm[...]
-    targets = ([down], [up], [(qkv, 0), (qkv, 1), (qkv, 2)], [(pair, 0), (pair, 1)], [out, cq, cout])
-    for s, pieces in enumerate(targets):
-        for half in range(2):
-            for way in range(2):
-                total = (ga[s][half, way].astype(F32) + gb[s][half, way].astype(F32)) * factor
-                width = total.shape[1] // len(pieces)
-                for p, target in enumerate(pieces):
-                    ref, slot = target if isinstance(target, tuple) else (target, 0)
-                    column = slot * 4 * width + (2 * half + way) * width
-                    ref[:, column:column + width] = total[:, p * width:(p + 1) * width]
+def finish_kernel(factor, lo, dt, dm, vec, *refs):
+    ga, gb = refs[:4], refs[4:8]
+    lo_out, dt_out, dm_out, qkv, out, cq, pair, cout, up, down, bias, up_bias, gain, shift = refs[8:]
+    lo_out[:, 0] = lo[...]
+    dt_out[:, 0] = dt[...]
+    dm_out[:, 0] = dm[...]
+    firsts = ((qkv, 0), (qkv, 1), (qkv, 2), (pair, 0), (pair, 1))
+    others = ((out, 0), (cq, 0), (cout, 0))
+    for half in range(2):
+        for way in range(2):
+            totals = [(a[half, way].astype(F32) + b[half, way].astype(F32)) * factor for a, b in zip(ga, gb)]
+            block, width = totals[0].shape[0], totals[3].shape[1] // len(others)
+            quarter = (2 * half + way) * width
+            for n in range(totals[0].shape[1] // width):
+                down[n * block:(n + 1) * block, quarter:quarter + width] = totals[0][:, n * width:(n + 1) * width]
+            wide = totals[1].shape[1]
+            up[:, (2 * half + way) * wide:(2 * half + way + 1) * wide] = totals[1]
+            for total, places in ((totals[2], firsts), (totals[3], others)):
+                for n, (ref, slot) in enumerate(places):
+                    column = slot * 4 * width + quarter
+                    ref[:, column:column + width] = total[:, n * width:(n + 1) * width]
+    at = lax.axis_index("dp")
+    d_model, width = vec.shape[1], bias.shape[1]
+    sums = vec[...] * factor
+    own = pltpu.roll(sums, lax.rem(d_model - at * width, d_model), 1)[:, :width]
+    bias[...] = own[0:7]
+    gain[...] = own[11:14]
+    shift[...] = own[14:17]
+    start = at * 4 * width
+    rows = lax.broadcasted_iota(jnp.int32, (4, d_model), 0)
+    row = jnp.sum(jnp.where(rows == lax.div(start, d_model), sums[7:11], 0.0), axis=0, keepdims=True)
+    row = jnp.broadcast_to(row, (8, d_model))
+    up_bias[...] = pltpu.roll(row, lax.rem(d_model - lax.rem(start, d_model), d_model), 1)[0:1, :4 * width]
 
 
 def finish_fused(settled, factor, d_model, ff):
-    lo, dt, dm, vec_sums = settled[:4]
+    lo, dt, dm = settled[:3]
     size = lax.axis_size("dp")
     block = d_model // size
-    rows = [jax.ShapeDtypeStruct(a.shape, BF16) for a in (lo, dt, dm)]
-    grads = [jax.ShapeDtypeStruct((block, n * d_model), F32) for n in (3, 1, 1, 2, 1)]
-    grads += [jax.ShapeDtypeStruct((block, ff), F32), jax.ShapeDtypeStruct((ff // size, d_model), F32)]
-    vmem = pl.BlockSpec(memory_space=pltpu.VMEM)
+    shapes = [jax.ShapeDtypeStruct((2, 1, *a.shape[1:]), BF16) for a in (lo, dt, dm)]
+    shapes += [jax.ShapeDtypeStruct((block, n * d_model), F32) for n in (3, 1, 1, 2, 1)]
+    shapes += [jax.ShapeDtypeStruct((block, ff), F32), jax.ShapeDtypeStruct((ff // size, d_model), F32)]
+    shapes += [jax.ShapeDtypeStruct(s, F32) for s in ((7, block), (1, ff // size), (3, block), (3, block))]
+
+    def whole(a):
+        return pl.BlockSpec(a.shape, lambda i: (0,) * len(a.shape))
+
     done = pl.pallas_call(
         functools.partial(finish_kernel, factor),
-        out_shape=rows + grads,
-        in_specs=[vmem] * 13,
-        out_specs=[vmem] * 10,
-        compiler_params=pltpu.CompilerParams(vmem_limit_bytes=32 * 1024 * 1024),
+        grid=(1,),
+        out_shape=shapes,
+        in_specs=[whole(a) for a in settled],
+        out_specs=[whole(s) for s in shapes],
+        compiler_params=pltpu.CompilerParams(vmem_limit_bytes=63 * 1024 * 1024),
         name="finish",
-    )(lo, dt, dm, *settled[4:])
-    vec_sums = jnp.concatenate([vec_sums, jnp.zeros((8, d_model), F32)], axis=0) * factor
-    return (done[0][:, None], done[1][:, None], done[2][:, None], *done[3:], *unpack_vectors(vec_sums, d_model))
+    )(*settled)
+    return (*done[:11], done[11][0], *done[12:])
 
 
 def pack_vectors(proj_bias, up_bias, norm_gain, norm_bias, d_model):
@@ -985,9 +1084,11 @@
 
     weights = [lax.all_gather(shard, "dp", axis=0, tiled=True) for shard in shards]
     vec_all = lax.psum(packed, "dp")[None]
-    bounds = lax.psum(counts[:, 0, 0], "seq")[micro]
+    counts = jnp.pad(lax.psum(counts, "seq")[micro][None], ((0, 31), (0, 0)))
+    place = jnp.full((8, 128), lax.axis_index("seq") % MB, jnp.int32)
+    counts = jnp.concatenate([counts, place], axis=0)
     w_all = jnp.concatenate(weights[:6], axis=1)
-    return whole(tokens), whole(memory), whole(cotangent), bounds, vec_all, w_all, weights[6]
+    return whole(tokens), whole(memory), whole(cotangent), counts, vec_all, w_all, weights[6]
 
 
 def own_rows(rows, core):
@@ -1036,29 +1137,25 @@
     self_qkv, self_out, cross_q, cross_kv, cross_out, ffn_up, ffn_down, proj_bias, up_bias, norm_gain, norm_bias,
 ):
     d_model = tokens.shape[3]
-    place = lax.axis_index("seq")
-    core = place % MB
     shards = (self_qkv, self_out, cross_q, cross_kv, cross_out, ffn_up, ffn_down)
-    docs = jnp.arange(9)
-    tgt_counts = jnp.sum(tgt_segments[:, 0, :, None] < docs, axis=1, dtype=jnp.int32)
-    src_counts = jnp.sum(src_segments[:, 0, :, None] < docs[1:], axis=1, dtype=jnp.int32)
-    counts = jnp.concatenate([tgt_counts, src_counts], axis=1)
-    counts = jnp.pad(counts[:, None, None], ((0, 0), (0, 0), (0, 7), (0, 128 - counts.shape[1])))
-    packed = pack_vectors(proj_bias, up_bias, norm_gain, norm_bias, d_model)
-    size, rows = lax.axis_size("dp"), self_qkv.shape[0]
+    size, rows, ff = lax.axis_size("dp"), self_qkv.shape[0], ffn_up.shape[1]
     fused = rows % 64 == 0 and size & (size - 1) == 0 and size > 2
     factor = 1.0 / math.sqrt(MB * size * tokens.shape[2] * lax.axis_size("seq"))
     if fused:
+        vectors = (proj_bias, up_bias[None], norm_gain, norm_bias)
         x_full, m_full, ct_full, counts, vec_all, w_all, w_down = gather_fused(
+            tokens, memory, cotangent, tgt_segments, src_segments, vectors, shards)
+    else:
+        docs = jnp.arange(1, 9)
+        tgt_counts = jnp.sum(tgt_segments[:, 0, :, None] < docs, axis=1, dtype=jnp.int32)
+        src_counts = jnp.sum(src_segments[:, 0, :, None] < docs, axis=1, dtype=jnp.int32)
+        counts = jnp.pad(jnp.concatenate([tgt_counts, src_counts], axis=1), ((0, 0), (1, 111)))
+        packed = pack_vectors(proj_bias, up_bias, norm_gain, norm_bias, d_model)
+        x_full, m_full, ct_full, counts, vec_all, w_all, w_down = gather_plain(
             tokens, memory, cotangent, counts, packed, shards)
-        bounds = jnp.sum(counts.reshape(-1, 8, 128), axis=0)[0]
-    else:
-        x_full, m_full, ct_full, bounds, vec_all, w_all, w_down = gather_plain(
-            tokens, memory, cotangent, counts, packed, shards)
-    bounds = jnp.concatenate([core.astype(jnp.int32)[None], bounds[:19]])
-    results = run_layer(bounds, x_full, m_full, ct_full, vec_all, w_all, w_down)
+    results = run_layer(counts, x_full, m_full, ct_full, vec_all, w_all, w_down)
     if fused:
-        return finish_fused(settle_fused(x_full, m_full, w_all, results), factor, d_model, ffn_up.shape[1])
+        return finish_fused(settle_fused(x_full, m_full, w_all, results), factor, d_model, ff)
     return settle_plain(x_full, m_full, w_all, results, factor)
 
 

time: 244 us -> 205 us (0.84); the launches traced: 241 us -> 205 us
  local copies, waits for them, and re-layouts: 18.4 us -> 1.22 us
  Pallas kernels: 219 us -> 203 us
  other arithmetic: 2.62 us -> 0 us
    unnamed x34 -> x0, local copies, waits for them, and re-layouts: 14 us -> none
    pallas_call x1, Pallas kernels: 81.1 us -> 68 us  [run_layer(): pl.pallas_call(layer_kernel, out_shape=out_shape, grid_spec=pltpu.Prefetc...]
    pallas_call x1, Pallas kernels: 82.8 us -> 78.4 us  [settle_fused(): pl.pallas_call(functools.partial(settle_kernel, size, shapes), out_shape=...]
where the time goes in v3:
time: 205 us
  Pallas kernels  203 us (99%)
    pallas_call x1, Pallas kernels, settle_fused(): pl.pallas_call(functools.partial(settle_kernel, size, shapes), out_shape=...  78.4 us
    pallas_call x1, Pallas kernels, run_layer(): pl.pallas_call(layer_kernel, out_shape=out_shape, grid_spec=pltpu.Prefetc...  68 us
    pallas_call x1, Pallas kernels, gather_fused(): pl.pallas_call(functools.partial(gather_kernel, size, splits), out_shape=...  52.8 us
    pallas_call x1, Pallas kernels, finish_fused(): pl.pallas_call(functools.partial(finish_kernel, factor), grid=(1,), out_s...  4.24 us

profile of v3, /device:TPU:0, one launch (start us, length us, event | category | flops | bytes accessed | tf_op | source)
XLA Modules:
  0.0 205.5 jit_solution(7280708671910545514)
XLA Ops:
  0.6 1.2 broadcast_in_dim.3.up_bias
  1.9 52.8 %gather.1 = (bf16[1536,512]{1,0:T(8,128)(2,1)}, bf16[1024,512]{1,0:T(8,128)(2,1)}, bf16[1536,512]{1,0:T(8,128)(2,1)}, s32[40,128]{1,0:T(8,128)}, bf16[8,32,512]{...) custom-call(bf16[2,1,384,512]{3,2,1,0:T(8,128)(2,1)} %tokens.1, ...), custom_call_target="tpu_custom_call" | custom-call | tf_op jit(solution)/shard_map/gather/pallas_call | solution.py:586
  54.7 68.0 %layer.1 = (bf16[768,512]{1,0:T(8,128)(2,1)}, bf16[768,512]{1,0:T(8,128)(2,1)}, bf16[768,512]{1,0:T(8,128)(2,1)}, bf16[768,512]{1,0:T(8,128)(2,1)}, bf16[768,512...) custom-call(s32[40,128]{1,0:T(8,128)} %get-tuple-element.66.counts, ...), custom_call_target="tpu_custom_call" | custom-call | tf_op jit(solution)/shard_map/layer/pallas_call | solution.py:399
  122.7 78.4 %settle.1 = (bf16[2,384,512]{2,1,0:T(8,128)(2,1)}, bf16[2,384,512]{2,1,0:T(8,128)(2,1)}, bf16[2,256,512]{2,1,0:T(8,128)(2,1)}, f32[24,512]{1,0:T(8,128)}, bf16[2...) custom-call(bf16[1536,512]{1,0:T(8,128)(2,1)} %get-tuple-element.63., ...), custom_call_target="tpu_custom_call" | custom-call | tf_op jit(solution)/shard_map/settle/pallas_call | solution.py:990
  201.1 4.2 %finish.1 = (bf16[2,1,384,512]{3,2,1,0:T(8,128)(2,1)}, bf16[2,1,384,512]{3,2,1,0:T(8,128)(2,1)}, bf16[2,1,256,512]{3,2,1,0:T(8,128)(2,1)}, f32[64,1536]{1,0:T(8,...) custom-call(bf16[2,384,512]{2,1,0:T(8,128)(2,1)} %get-tuple-element., ...), custom_call_target="tpu_custom_call" | custom-call | tf_op jit(solution)/shard_map/finish/pallas_call | solution.py:1050
